TPU v7x, 32 devices: a whole 2x2x4 slice. The times are simulated.
32 devices in a mesh: seq: 8 (over z, x), dp: 4 (over y, core).
Axes of the slice: x: 2, y: 2, z: 4, core: 2. Of those that a mesh axis runs over, the one named last changes fastest.
Arguments:
- layer_input: bfloat16 [4, 2048, 768], P('dp', 'seq'), may hold values from -6 to 6
- out_cotangent: bfloat16 [4, 2048, 768], P('dp', 'seq'), may hold values from -6 to 6
- segment_ids: int32 [4, 2048], P('dp', 'seq'), may hold values from 0 to 2, as said below
- piece_owner: int32 [768], replicated, may hold values from 0 to 31, as said below
- weight_master: float32 [1024, 16, 768], P(('seq', 'dp'))
- weight_first: float32 [1024, 16, 768], P(('seq', 'dp'))
- weight_second: float32 [1024, 16, 768], P(('seq', 'dp'))
- norm_params: float32 [4, 768], replicated
- norm_first: float32 [4, 768], replicated
- norm_second: float32 [4, 768], replicated
Outputs:
- out_hidden: bfloat16 [4, 2048, 768], P('dp', 'seq')
- input_grad: float32 [4, 2048, 768], P('dp', 'seq')
- weight_grads: float32 [1024, 16, 768], P(('seq', 'dp'))
- weight_first_new: float32 [1024, 16, 768], P(('seq', 'dp'))
- weight_second_new: float32 [1024, 16, 768], P(('seq', 'dp'))
- weight_new: float32 [1024, 16, 768], P(('seq', 'dp'))
- weight_low: bfloat16 [1024, 16, 768], P(('seq', 'dp'))
- norm_grads: float32 [4, 768], replicated
- norm_first_new: float32 [4, 768], replicated
- norm_second_new: float32 [4, 768], replicated
- norm_new: float32 [4, 768], replicated
Inputs may be any that keep to these rules, and one draw needn't show every extreme that they name: `segment_ids`: in each sequence the numbers never fall: 0 on its first positions, 2 on its last ones, 1 between; the documents numbered 0 and 2 each hold 1 to 255 tokens. `piece_owner`: each device owns at most 32 pieces, and some device owns exactly 32.
All inputs are finite; a program needn't handle non-finite values.
Results may differ from a plain program's by a relative error of at most 0.013.
The roundings to bfloat16 on the way count: a program that leaves them out, or rounds other values in their place, can miss the bound.
Values may be sent and summed in bfloat16 or wider, within the bound.
A program may use at most 256 MiB of HBM per device.

v0:
```python
import functools

import jax
import jax.numpy as jnp
import numpy as np
from jax import lax
from jax.experimental import pallas as pl
from jax.experimental.pallas import tpu as pltpu
from jax.sharding import Mesh
from jax.sharding import PartitionSpec as P

HEADS = 12
GROUPS = 4
TRIO = HEADS // GROUPS
STEP = 4

NORM_EPS = 1e-06
BETA_ONE = 0.5
BETA_TWO = 0.5
DECAY = 0.01
ADAM_EPS = 1e-08
NORM_RATE = 0.3
OUT_RATE = 0.35
MASKED = -1e30
CHUNKS = 6
VMEM_LIMIT = 60 * 1024 * 1024
MESH_IDS = pl.DeviceIdType.MESH
F32 = jnp.float32
BF16 = jnp.bfloat16


def head_slopes(head_count, tok_rows, seq_devices):
    head_order = np.arange(head_count, dtype=np.float64)
    slopes = 8.0 / tok_rows * np.power(8.0 * seq_devices, -head_order / (head_count - 1))
    return slopes.astype(np.float32)


def locate_pieces(owners, slot_count):
    pieces = owners.shape[0]
    numbers = jnp.arange(pieces, dtype=jnp.int32)
    earlier = (owners[None, :] == owners[:, None]) & (numbers[None, :] < numbers[:, None])
    return owners * slot_count + jnp.sum(earlier.astype(jnp.int32), axis=1)


def slot_rates(inverse, piece_rows, model_width, hidden_units):
    first_row = (inverse - 1) * piece_rows
    narrow = model_width ** (-0.5)
    step_rate = jnp.where(
        first_row < 3 * model_width,
        narrow,
        jnp.where(
            first_row < 4 * model_width,
            OUT_RATE,
            jnp.where(
                first_row < 4 * model_width + 2 * hidden_units, narrow, hidden_units ** (-0.5)
            ),
        ),
    )
    return jnp.where(inverse > 0, step_rate, narrow).astype(jnp.float32)


def adamw_step(weight, first_moment, second, gradient, step_rate, step_count):
    first_moment = BETA_ONE * first_moment + (1.0 - BETA_ONE) * gradient
    second = BETA_TWO * second + (1.0 - BETA_TWO) * gradient * gradient
    mean_hat = first_moment / (1.0 - BETA_ONE**step_count)
    square_hat = second / (1.0 - BETA_TWO**step_count)
    weight = weight - step_rate * (mean_hat / (jnp.sqrt(square_hat) + ADAM_EPS) + DECAY * weight)
    return (first_moment, second, weight)


def dot_nt(left_side, right_side):
    return lax.dot_general(
        left_side, right_side, (((1,), (1,)), ((), ())), preferred_element_type=F32
    )


def dot_nn(left_side, right_side):
    return lax.dot_general(
        left_side, right_side, (((1,), (0,)), ((), ())), preferred_element_type=F32
    )


def dot_tn(left_side, right_side):
    return lax.dot_general(
        left_side, right_side, (((0,), (0,)), ((), ())), preferred_element_type=F32
    )


def fetch_piece(place, piece, weights, dst, sem):
    pltpu.make_async_copy(weights.at[place[piece]], dst, sem).start()


def fill_tables(table, slopes, group, tok):
    apart = lax.broadcasted_iota(jnp.int32, (tok, tok), 0) - lax.broadcasted_iota(
        jnp.int32, (tok, tok), 1
    )
    apart = apart.astype(F32)
    for h in range(TRIO):
        slope = slopes[group * TRIO + h]
        table[h * 3 + 0] = -slope * apart
        table[h * 3 + 1] = slope * jnp.abs(apart)
        table[h * 3 + 2] = slope * apart


def block_place(order, n_dp, reps):
    return (order % n_dp) * reps + order // n_dp


def bias_of(key_block, query_place, slope, h, tok, n_dp, reps):
    key_place = block_place(key_block, n_dp, reps)
    which = jnp.where(key_place > query_place, 2, jnp.where(key_place < query_place, 0, 1))
    shift = slope * (tok * jnp.abs(key_place - query_place)).astype(F32)
    return h * 3 + which, shift


def holder(order, n_dp):
    dp = lax.rem(order, n_dp)
    return {"b": lax.div(order, n_dp), "y": lax.div(dp, 2), "core": lax.rem(dp, 2)}


def turn_to():
    z, dp = lax.axis_index("a"), lax.axis_index("y") * 2 + lax.axis_index("core")
    return {"a": dp, "y": lax.div(z, 2), "core": lax.rem(z, 2)}, dp != z


def start_turn(src, dst, send_sem, recv_sem):
    peer, moves = turn_to()

    @pl.when(moves)
    def _():
        pltpu.make_async_remote_copy(
            src_ref=src,
            dst_ref=dst,
            send_sem=send_sem,
            recv_sem=recv_sem,
            device_id=peer,
            device_id_type=MESH_IDS,
        ).start()

    @pl.when(jnp.logical_not(moves))
    def _():
        pltpu.make_async_copy(src, dst, recv_sem).start()


def finish_turn(src, dst, send_sem, recv_sem):
    peer, moves = turn_to()

    @pl.when(moves)
    def _():
        pltpu.make_async_remote_copy(
            src_ref=src,
            dst_ref=dst,
            send_sem=send_sem,
            recv_sem=recv_sem,
            device_id=peer,
            device_id_type=MESH_IDS,
        ).wait()

    @pl.when(jnp.logical_not(moves))
    def _():
        pltpu.make_async_copy(src, dst, recv_sem).wait()


def greet(peers, turning=False, meanwhile=None):
    barrier = pltpu.get_barrier_semaphore()
    for peer in peers:
        pl.semaphore_signal(barrier, inc=1, device_id=peer, device_id_type=MESH_IDS)
    if meanwhile is not None:
        meanwhile()
    if not turning:
        pl.semaphore_wait(barrier, len(peers))
        return
    turn_peer, moves = turn_to()

    @pl.when(moves)
    def _():
        pl.semaphore_signal(barrier, inc=1, device_id=turn_peer, device_id_type=MESH_IDS)

    pl.semaphore_wait(barrier, len(peers) + moves.astype(jnp.int32))


def my_order(n_dp):
    return lax.axis_index("b") * n_dp + lax.axis_index("y") * 2 + lax.axis_index("core")


def remote(src, dst, sems, index, peer):
    return pltpu.make_async_remote_copy(
        src_ref=src,
        dst_ref=dst,
        send_sem=sems.at[0, index],
        recv_sem=sems.at[1, index],
        device_id=peer,
        device_id_type=MESH_IDS,
    )


def project_kernel(
    sizes,
    place,
    x_ref,
    weights,
    q_out,
    k_out,
    kt_out,
    v_out,
    vt_out,
    wpad,
    sems,
):
    n_dp, splits, tok, head = sizes
    order = my_order(n_dp)
    group, split = lax.div(order, splits), lax.rem(order, splits)
    block = pl.program_id(0)
    per_head = head // 16
    width = x_ref.shape[2]
    kind_pieces = width // 16

    @pl.when(block == 0)
    def _():
        def spots():
            for kind in range(3):
                for rest in range(TRIO * per_head):
                    step = kind * TRIO * per_head + rest
                    rows = pl.ds(rest % per_head * 16, 16)
                    dst = wpad.at[kind * TRIO + rest // per_head, rows]
                    yield kind * kind_pieces + group * (TRIO * per_head) + rest, dst, sems.at[step]

        for number, dst, sem in spots():
            fetch_piece(place, number, weights, dst, sem)
        for row in range(3 * TRIO):
            wpad[row, head:, :] = jnp.zeros((wpad.shape[1] - head, width), BF16)
        for _, dst, sem in spots():
            pltpu.make_async_copy(weights.at[0], dst, sem).wait()

    segs = x_ref[0, tok : tok + 1, 0:tok].astype(F32)
    number = lax.broadcasted_iota(jnp.int32, (128, tok), 0) - head
    same = segs == number.astype(F32)
    used = (number >= 0) & (number < 3)
    xb = x_ref[0, 0:tok, :]
    keys = dot_nt(xb, wpad[TRIO : 2 * TRIO].reshape(TRIO * 128, width))
    values = dot_nt(xb, wpad[2 * TRIO : 3 * TRIO].reshape(TRIO * 128, width))
    marks = jnp.where(used & jnp.logical_not(same), MASKED, 0.0).T.astype(BF16)
    for h in range(TRIO):
        key = keys[:, h * 128 : (h + 1) * 128]
        value = values[:, h * 128 : (h + 1) * 128]
        k_out[h] = key.astype(BF16) + marks
        v_out[h] = value[:, 0:head].astype(BF16)
        kt_out[h] = key.T[0:head].astype(BF16)
        vt_out[h] = value.T[0:head].astype(BF16)

    @pl.when(lax.rem(block, splits) == split)
    def _():
        w_query = wpad[0:TRIO].reshape(TRIO * 128, width)
        queries = dot_nt(xb, w_query).astype(BF16) * jnp.asarray(head**-0.5, BF16)
        query_marks = jnp.where(same & used, 1.0, 0.0).T.astype(BF16)
        for h in range(TRIO):
            q_out[h] = queries[:, h * 128 : (h + 1) * 128] + query_marks


def attend_forward_kernel(
    sizes,
    slopes,
    q_ref,
    k_ref,
    vt_ref,
    cot_in,
    mixed_full,
    log_out,
    mixed_own,
    cot_out,
    table,
    scores,
    mixed_low,
    swap_sems,
    turn_sems,
):
    n_dp, reps, splits, tok, head, blocks = sizes
    order = my_order(n_dp)
    group, split = lax.div(order, splits), lax.rem(order, splits)
    others = [lax.rem(group + k, GROUPS) for k in range(1, GROUPS)]
    peers = [holder(other * splits + split, n_dp) for other in others]
    started = []
    greet(peers, True)
    turn_refs = (cot_in, cot_out, turn_sems.at[0], turn_sems.at[1])
    start_turn(*turn_refs)
    fill_tables(table, slopes, group, tok)

    def attend(index, h):
        place_order = index * splits + split
        query_place = lax.rem(place_order, n_dp) * reps + lax.div(place_order, n_dp)
        slope = slopes[group * TRIO + h]
        qh = q_ref[h, pl.ds(pl.multiple_of(index * tok, tok), tok), :]
        top = None
        shifts = []
        for kb in range(blocks):
            which, shift = bias_of(kb, query_place, slope, h, tok, n_dp, reps)
            now = dot_nt(k_ref[h, kb * tok : (kb + 1) * tok, :], qh) - table[which]
            scores[kb] = now
            here = jnp.max(now, axis=0, keepdims=True) - shift
            top = here if top is None else jnp.maximum(top, here)
            shifts.append(shift)
        total = jnp.zeros((1, tok), F32)
        for kb in range(blocks):
            grown = jnp.exp(scores[kb] - (top + shifts[kb]))
            total = total + jnp.sum(grown, axis=0, keepdims=True)
            scores[kb] = grown
        inverse = 1.0 / total
        mixed = jnp.zeros((head, tok), F32)
        for kb in range(blocks):
            prob = (scores[kb] * inverse).astype(BF16)
            mixed = mixed + dot_nn(vt_ref[h, :, kb * tok : (kb + 1) * tok], prob)
        mixed_full[index, h] = mixed
        mixed_low[index, h] = mixed.astype(BF16)
        log_out[index, h] = top + jnp.log(total)

    for k in list(range(GROUPS - 1)) + [None]:
        index = group if k is None else others[k]

        def one(h, carry, index=index):
            attend(index, h)
            return carry

        lax.fori_loop(0, TRIO, one, None)
        if k is not None:
            copy = swap_copy(mixed_low, mixed_own, index, group, swap_sems, k, peers[k])
            copy.start()
            started.append(copy)
        else:
            mixed_own[group] = mixed_low[group]
    for copy in started:
        copy.wait()
    finish_turn(*turn_refs)


def swap_copy(src, dst, there, here, sems, index, peer):
    return pltpu.make_async_remote_copy(
        src_ref=src.at[there],
        dst_ref=dst.at[here],
        send_sem=sems.at[0, index],
        recv_sem=sems.at[1, index],
        device_id=peer,
        device_id_type=MESH_IDS,
    )


def norm_steps(dims, norm_in, norm_out, refs):
    zn, xn, yn = dims
    norm_core, norm_y, norm_x, norm_z, norm_sum, sems = refs
    z, x = lax.axis_index("a"), lax.axis_index("b")
    y, core = lax.axis_index("y"), lax.axis_index("core")
    rounds = [
        (norm_core, [{"core": 1 - core}]),
        (norm_y, [{"y": lax.rem(y + k, yn)} for k in range(1, yn)]),
        (norm_x, [{"b": lax.rem(x + k, xn)} for k in range(1, xn)]),
        (norm_z, [{"a": lax.rem(z + k, zn)} for k in range(1, zn)]),
    ]
    first = [sum(len(peers) for _, peers in rounds[:i]) for i in range(len(rounds))]

    def copies(i):
        buffer, peers = rounds[i]
        return [
            remote(norm_sum.at[i], buffer.at[k], sems, first[i] + k, peer)
            for k, peer in enumerate(peers)
        ]

    def begin():
        norm_sum[0] = norm_in[...]
        for copy in copies(0):
            copy.start()

    def turn_round(i):
        total = norm_sum[i]
        for k, copy in enumerate(copies(i)):
            copy.wait()
            total = total + rounds[i][0][k]
        if i + 1 == len(rounds):
            norm_out[...] = total
            return
        norm_sum[i + 1] = total
        for copy in copies(i + 1):
            copy.start()

    peers = [peer for _, group in rounds for peer in group]
    return peers, [begin] + [functools.partial(turn_round, i) for i in range(len(rounds))]


def attend_backward_kernel(
    sizes,
    slopes,
    q_ref,
    k_ref,
    kt_ref,
    v_ref,
    mixed_full,
    log_in,
    d_mixed,
    low_in,
    norm_in,
    own_ref,
    low_out,
    norm_out,
    dk_sum,
    dv_sum,
    table,
    d_blocks,
    shared,
    pairs,
    landed,
    swap_sems,
    query_sems,
    pair_sems,
    value_sems,
    turn_sems,
    *norm_refs,
):
    n_dp, reps, splits, tok, head, blocks = sizes
    order = my_order(n_dp)
    group, split = lax.div(order, splits), lax.rem(order, splits)
    twins = [lax.rem(split + k, splits) for k in range(1, splits)]
    twin_ids = [holder(group * splits + other, n_dp) for other in twins]
    others = [lax.rem(group + k, GROUPS) for k in range(1, GROUPS)]
    peers = [holder(other * splits + split, n_dp) for other in others]
    norm_peers, norms = norm_steps((n_dp, reps, n_dp // 2), norm_in, norm_out, norm_refs)
    greet(twin_ids + peers + norm_peers, True)
    turn_refs = (low_in, low_out, turn_sems.at[0], turn_sems.at[1])
    started = []

    def launch(copy):
        copy.start()
        started.append(copy)

    for k in range(GROUPS - 1):
        launch(remote(d_mixed.at[others[k]], d_blocks.at[group], swap_sems, k, peers[k]))
    d_blocks[group] = d_mixed[group]
    norms.pop(0)()
    fill_tables(table, slopes, group, tok)
    dk_sum[...] = jnp.zeros_like(dk_sum)
    dv_sum[...] = jnp.zeros_like(dv_sum)

    def step_fn(h, step):
        index = lax.rem(group + GROUPS - step, GROUPS)
        if h == 0:

            @pl.when(step > 0)
            def _():
                view = d_blocks.at[index]
                remote(view, view, swap_sems, step - 1, peers[0]).wait_recv()

        place_order = index * splits + split
        query_place = lax.rem(place_order, n_dp) * reps + lax.div(place_order, n_dp)
        slope = slopes[group * TRIO + h]
        qh = q_ref[h, pl.ds(pl.multiple_of(index * tok, tok), tok), :]
        dt = d_blocks[index, h]
        row_dot = jnp.sum(dt.astype(F32) * mixed_full[index, h], axis=0, keepdims=True)
        log_total = log_in[index, h]
        dq = jnp.zeros((head, tok), F32)
        for kb in range(blocks):
            rows = slice(kb * tok, (kb + 1) * tok)
            which, shift = bias_of(kb, query_place, slope, h, tok, n_dp, reps)
            now = dot_nt(k_ref[h, rows, :], qh) - table[which]
            prob = jnp.exp(now - (log_total + shift))
            d_prob = dot_nn(v_ref[h, rows, :], dt)
            d_score = (prob * (d_prob - row_dot)).astype(BF16)
            dv_sum[rows, :] += dot_nt(prob.astype(BF16), dt)
            dk_sum[rows, :] += dot_nn(d_score, qh)
            dq = dq + dot_nn(kt_ref[h, :, rows], d_score)
        shared[index, 0, h] = (dq * (head**-0.5)).astype(BF16)

    def pair_copy(h, k):
        return remote(
            pairs.at[h, twins[k]], landed.at[h, k], pair_sems, h * (splits - 1) + k, twin_ids[k]
        )

    def take_pairs(h):
        for k in range(splits - 1):
            pair_copy(h, k).wait_recv()
        for index in range(GROUPS):
            for kind in range(2):
                total = pairs[h, split, index, kind].astype(F32)
                for k in range(splits - 1):
                    total = total + landed[h, k, index, kind].astype(F32)
                shared[index, kind + 1, h] = total.astype(BF16)
        for k in range(GROUPS - 1):
            launch(
                remote(
                    shared.at[others[k], pl.ds(1, 2), h],
                    own_ref.at[group, pl.ds(1, 2), h],
                    value_sems,
                    h * (GROUPS - 1) + k,
                    peers[k],
                )
            )

    for h in range(TRIO):

        def one(step, carry, h=h):
            step_fn(h, step)
            return carry

        lax.fori_loop(0, GROUPS, one, None)
        if h == 0:
            start_turn(*turn_refs)
        norms.pop(0)()
        for k in range(GROUPS - 1):
            launch(
                remote(
                    shared.at[others[k], 0, h],
                    own_ref.at[group, 0, h],
                    query_sems,
                    h * (GROUPS - 1) + k,
                    peers[k],
                )
            )

        def flip(index, carry, h=h):
            for part in range(splits):
                rows = pl.ds(pl.multiple_of((index * splits + part) * tok, tok), tok)
                pairs[h, part, index, 0] = dk_sum[rows, :].T[0:head].astype(BF16)
                pairs[h, part, index, 1] = dv_sum[rows, :].T.astype(BF16)
            return carry

        lax.fori_loop(0, GROUPS, flip, None)
        if h + 1 < TRIO:
            dk_sum[...] = jnp.zeros_like(dk_sum)
            dv_sum[...] = jnp.zeros_like(dv_sum)
        for k in range(splits - 1):
            launch(pair_copy(h, k))
        if h > 0:
            take_pairs(h - 1)
    for step in norms:
        step()
    take_pairs(TRIO - 1)
    own_ref[group] = shared[group]
    for h in range(TRIO):
        for k in range(GROUPS - 1):
            view = own_ref.at[others[k], 0, h]
            remote(view, view, query_sems, h * (GROUPS - 1) + k, peers[k]).wait_recv()
            view = own_ref.at[others[k], pl.ds(1, 2), h]
            remote(view, view, value_sems, h * (GROUPS - 1) + k, peers[k]).wait_recv()
    finish_turn(*turn_refs)
    for copy in started:
        copy.wait_send()


def norm_stats(values_in):
    mean = jnp.mean(values_in, axis=-1, keepdims=True)
    centred = values_in - mean
    spread = jnp.mean(centred * centred, axis=-1, keepdims=True)
    scale = lax.rsqrt(spread + NORM_EPS)
    return centred * scale, scale


def norm_back(unit, scale, gain, cotangent):
    d_unit = cotangent * gain
    first = jnp.mean(d_unit, axis=-1, keepdims=True)
    second = jnp.mean(d_unit * unit, axis=-1, keepdims=True)
    d_in = scale * (d_unit - first - unit * second)
    d_gain = jnp.sum(cotangent * unit, axis=0, keepdims=True)
    d_bias = jnp.sum(cotangent, axis=0, keepdims=True)
    return d_in, d_gain, d_bias


def dense_kernel(
    sizes,
    place,
    gathered,
    cot_ref,
    mixed_ref,
    norm_ref,
    weights,
    out_ref,
    d_pre_one_ref,
    d_mixed_ref,
    norm_grad,
    grads,
    w_out,
    w_gate,
    w_up,
    w_down,
    keep_gate,
    keep_up,
    keep_hidden,
    stage,
    stage_out,
    x_ref,
    load_sems,
    store_sems,
    own_sem,
):
    n_dp, tok, piece, kind_pieces, chunk_pieces, hidden_pieces = sizes
    own_copy = pltpu.make_async_copy(
        gathered.at[my_order(n_dp), pl.ds(0, tok)], x_ref, own_sem
    )
    own_copy.start()
    first_gate = 4 * kind_pieces
    first_up = first_gate + hidden_pieces
    first_down = first_up + hidden_pieces
    bases = (first_gate, first_up, first_down)
    buffers = (w_gate, w_up, w_down)
    chunk = chunk_pieces * piece

    for step in range(kind_pieces):
        dst = w_out.at[pl.ds(step * piece, piece)]
        fetch_piece(place, 3 * kind_pieces + step, weights, dst, load_sems.at[3 * CHUNKS])

    def load_chunk(c):
        for step in range(chunk_pieces):
            for kind in range(3):
                dst = buffers[kind].at[c, pl.ds(step * piece, piece)]
                number = bases[kind] + c * chunk_pieces + step
                fetch_piece(place, number, weights, dst, load_sems.at[kind * CHUNKS + c])

    def wait_chunk(c):
        for kind in range(3):
            view = buffers[kind].at[c]
            pltpu.make_async_copy(view, view, load_sems.at[kind * CHUNKS + c]).wait()

    load_chunk(0)
    mixed = mixed_ref[...].T
    own_copy.wait()
    pltpu.make_async_copy(w_out, w_out, load_sems.at[3 * CHUNKS]).wait()
    pre_one = x_ref[...].astype(F32) + dot_nt(mixed, w_out[...])
    load_chunk(1)
    unit_one, scale_one = norm_stats(pre_one)
    h_one = unit_one * norm_ref[0:1, :] + norm_ref[1:2, :]
    h_low = h_one.astype(BF16)

    pre_two = h_one
    for c in range(CHUNKS):
        wait_chunk(c)
        gate = dot_nt(w_gate[c], h_low)
        up = dot_nt(w_up[c], h_low)
        if c + 2 < CHUNKS:
            load_chunk(c + 2)
        below = 0.5 * (1.0 + lax.erf(gate * (0.5**0.5)))
        gelu = gate * below
        slope = below + gate * (jnp.exp(-0.5 * gate * gate) * (0.5 / jnp.pi) ** 0.5)
        hidden = (gelu * up).astype(BF16)
        keep_gate[c] = up * slope
        keep_up[c] = gelu
        keep_hidden[c] = hidden
        pre_two = pre_two + dot_tn(hidden, w_down[c])

    unit_two, scale_two = norm_stats(pre_two)
    out_ref[...] = (unit_two * norm_ref[2:3, :] + norm_ref[3:4, :]).astype(BF16)
    d_pre_two, d_gain_two, d_bias_two = norm_back(
        unit_two, scale_two, norm_ref[2:3, :], cot_ref[...].astype(F32)
    )
    d_branch = d_pre_two.astype(BF16)

    def drain(slot):
        for kind in range(3):
            view = stage.at[slot, kind]
            pltpu.make_async_copy(view, view, store_sems.at[slot * 3 + kind]).wait()

    d_h = d_pre_two
    for c in range(CHUNKS):
        slot = c % 2
        if c >= 2:
            drain(slot)
        d_hidden = dot_nt(w_down[c], d_branch)
        d_gate = (d_hidden * keep_gate[c]).astype(BF16)
        d_up = (d_hidden * keep_up[c]).astype(BF16)
        stage[slot, 0] = dot_nn(d_gate, h_low).astype(BF16)
        stage[slot, 1] = dot_nn(d_up, h_low).astype(BF16)
        stage[slot, 2] = dot_nn(keep_hidden[c], d_branch).astype(BF16)
        for step in range(chunk_pieces):
            for kind in range(3):
                pltpu.make_async_copy(
                    stage.at[slot, kind, pl.ds(step * piece, piece)],
                    grads.at[place[bases[kind] + c * chunk_pieces + step]],
                    store_sems.at[slot * 3 + kind],
                ).start()
        d_h = d_h + dot_tn(d_gate, w_gate[c]) + dot_tn(d_up, w_up[c])

    d_pre_one, d_gain_one, d_bias_one = norm_back(unit_one, scale_one, norm_ref[0:1, :], d_h)
    d_pre_one_ref[...] = d_pre_one
    d_proj = d_pre_one.astype(BF16)
    stage_out[...] = dot_tn(d_proj, mixed).astype(BF16)
    for step in range(kind_pieces):
        pltpu.make_async_copy(
            stage_out.at[pl.ds(step * piece, piece)],
            grads.at[place[3 * kind_pieces + step]],
            store_sems.at[6],
        ).start()
    d_mixed_ref[...] = lax.dot_general(
        w_out[...], d_proj, (((0,), (1,)), ((), ())), preferred_element_type=F32
    ).astype(BF16)
    norm_grad[...] = jnp.concatenate(
        [
            d_gain_one,
            d_bias_one,
            d_gain_two,
            d_bias_two,
            jnp.zeros((4, d_gain_one.shape[1]), F32),
        ],
        axis=0,
    )
    drain(CHUNKS % 2)
    drain((CHUNKS + 1) % 2)
    pltpu.make_async_copy(stage_out, stage_out, store_sems.at[6]).wait()


def project_grad_kernel(
    sizes,
    place,
    gathered,
    d_own,
    d_pre_one,
    weights,
    grads_in,
    d_input,
    grads,
    w_all,
    stage,
    x_ref,
    load_sems,
    store_sems,
    own_sem,
):
    n_dp, tok, piece, kind_pieces = sizes
    own_copy = pltpu.make_async_copy(
        gathered.at[my_order(n_dp), pl.ds(0, tok)], x_ref, own_sem
    )
    own_copy.start()
    group_pieces = kind_pieces // GROUPS
    del grads_in

    def each(group):
        for kind in range(3):
            for step in range(group_pieces):
                row = (kind * group_pieces + step) * piece
                yield kind * kind_pieces + group * group_pieces + step, pl.ds(row, piece)

    def load(group):
        for number, span in each(group):
            fetch_piece(place, number, weights, w_all.at[group, span], load_sems.at[group])

    load(0)
    load(1)
    own_copy.wait()
    x_own = x_ref[...]
    for group in range(GROUPS):
        stage[group] = dot_nn(d_own[group], x_own).astype(BF16)
        if group + 2 < GROUPS:
            load(group + 2)
        for number, span in each(group):
            pltpu.make_async_copy(
                stage.at[group, span], grads.at[place[number]], store_sems.at[group]
            ).start()
    total = d_pre_one[...]
    for group in range(GROUPS):
        view = w_all.at[group]
        pltpu.make_async_copy(view, view, load_sems.at[group]).wait()
        total = total + dot_tn(d_own[group], w_all[group])
    d_input[...] = total.astype(BF16)
    for group in range(GROUPS):
        view = stage.at[group]
        pltpu.make_async_copy(view, view, store_sems.at[group]).wait()


def add_low(dst, src, rows):
    def one(i, carry):
        dst[i] = (dst[i].astype(F32) + src[i].astype(F32)).astype(BF16)
        return carry

    lax.fori_loop(0, rows, one, None)


def z_order_of(count):
    order = [0]
    for k in range(1, count):
        for far in (k, count - k):
            if far not in order:
                order.append(far)
    return order


def spread_steps(sizes, own, every, sems):
    zn, xn, yn, slots, last = sizes
    z_sems, xs_sems, ys_sems, xf_sems, yf_sems, near_sems, own_sem = sems[:7]
    xb_sems, yb_sems, zb_sems, nb_sems = sems[7:11]
    count = slots - last
    part = count * 9 // 16
    rest = count - part
    z, x = lax.axis_index("a"), lax.axis_index("b")
    y, core = lax.axis_index("y"), lax.axis_index("core")
    core_peer = {"core": 1 - core}
    xs, ys, z_order = range(1, xn), range(1, yn), z_order_of(zn)
    x_peers = {k: {"b": lax.rem(x + k, xn)} for k in xs}
    y_peers = {k: {"y": lax.rem(y + k, yn)} for k in ys}
    z_peers = {k: {"a": lax.rem(z + k, zn)} for k in range(1, zn)}
    source = own.at[pl.ds(0, count)]

    def number(jz, jx, jy):
        chip = (lax.rem(z + zn - jz, zn) * xn + lax.rem(x + xn - jx, xn)) * yn + lax.rem(
            y + yn - jy, yn
        )
        return chip * 2 + core

    def shard(jz, jx, jy, lead=0, rows=count):
        return every.at[pl.ds(number(jz, jx, jy) * slots + lead, rows)]

    def tail(jz, jx, jy):
        return shard(jz, jx, jy, count, last)

    def tail_held(jz, jx, jy):
        return own.at[pl.ds(count, last)] if (jz, jx, jy) == (0, 0, 0) else tail(jz, jx, jy)

    def xb_copy(jx, jy):
        index = (jx - 1) * yn + jy
        return remote(tail_held(0, 0, jy), tail(0, 0, jy), xb_sems, index, x_peers[jx])

    def yb_copy(jy):
        return remote(tail_held(0, 0, 0), tail(0, 0, 0), yb_sems, jy - 1, y_peers[jy])

    def zb_copy(jz, jx, jy):
        index = ((jz - 1) * xn + jx) * yn + jy
        return remote(tail_held(0, jx, jy), tail(0, jx, jy), zb_sems, index, z_peers[jz])

    def nb_copy(jz, jx, jy):
        index = (jz * xn + jx) * yn + jy
        return remote(tail_held(jz, jx, jy), tail(jz, jx, jy), nb_sems, index, core_peer)

    def tail_begin():
        for jy in ys:
            launch(yb_copy(jy))
        for jx in xs:
            launch(xb_copy(jx, 0))
        launch(nb_copy(0, 0, 0))

    def tail_across():
        for jy in ys:
            view = tail(0, 0, jy)
            remote(view, view, yb_sems, jy - 1, y_peers[jy]).wait_recv()
            for jx in xs:
                launch(xb_copy(jx, jy))
            launch(nb_copy(0, 0, jy))

    def tail_planes():
        for jx in xs:
            for jy in range(yn):
                view = tail(0, jx, jy)
                remote(view, view, xb_sems, (jx - 1) * yn + jy, x_peers[jx]).wait_recv()
                launch(nb_copy(0, jx, jy))
        for jz in z_order[1:]:
            for jx in range(xn):
                for jy in range(yn):
                    launch(zb_copy(jz, jx, jy))

    def tail_end():
        for jz in z_order[1:]:
            for jx in range(xn):
                for jy in range(yn):
                    view = tail(jz, jx, jy)
                    index = ((jz - 1) * xn + jx) * yn + jy
                    remote(view, view, zb_sems, index, z_peers[jz]).wait_recv()
                    launch(nb_copy(jz, jx, jy))

    def tail_settle():
        for jz in range(zn):
            for jx in range(xn):
                for jy in range(yn):
                    chip = lax.div(number(jz, jx, jy), 2)
                    view = every.at[pl.ds((chip * 2 + 1 - core) * slots + count, last)]
                    index = (jz * xn + jx) * yn + jy
                    remote(view, view, nb_sems, index, core_peer).wait_recv()

    def held(jz, jx, jy):
        return source if (jz, jx, jy) == (0, 0, 0) else shard(jz, jx, jy)

    def z_copy(jz):
        return remote(source, shard(0, 0, 0), z_sems, jz - 1, z_peers[jz])

    def xs_copy(jz, jx):
        return remote(
            held(jz, 0, 0), shard(jz, 0, 0), xs_sems, jz * (xn - 1) + jx - 1, x_peers[jx]
        )

    def ys_copy(jz, jy):
        return remote(
            held(jz, 0, 0), shard(jz, 0, 0), ys_sems, jz * (yn - 1) + jy - 1, y_peers[jy]
        )

    def cross(jz, jx, jy):
        return (jz * (xn - 1) + jx - 1) * (yn - 1) + jy - 1

    def xf_copy(jz, jx, jy):
        view = shard(jz, 0, jy, part, rest)
        return remote(view, view, xf_sems, cross(jz, jx, jy), x_peers[jx])

    def yf_copy(jz, jx, jy):
        view = shard(jz, jx, 0, 0, part)
        return remote(view, view, yf_sems, cross(jz, jx, jy), y_peers[jy])

    def near_copy(jz, jx, jy):
        return remote(
            held(jz, jx, jy),
            shard(jz, jx, jy),
            near_sems,
            (jz * xn + jx) * yn + jy,
            core_peer,
        )

    started = []

    def launch(copy):
        copy.start()
        started.append(copy)

    def send_own(jz):
        for jx in xs:
            launch(xs_copy(jz, jx))
        for jy in ys:
            launch(ys_copy(jz, jy))
        launch(near_copy(jz, 0, 0))

    def ys_copy_in(jz, jy):
        view = shard(jz, 0, jy)
        remote(view, view, ys_sems, jz * (yn - 1) + jy - 1, y_peers[jy]).wait_recv()

    def xs_copy_in(jz, jx):
        view = shard(jz, jx, 0)
        remote(view, view, xs_sems, jz * (xn - 1) + jx - 1, x_peers[jx]).wait_recv()

    def forward(jz):
        for jy in ys:
            ys_copy_in(jz, jy)
            for jx in xs:
                launch(xf_copy(jz, jx, jy))
        for jx in xs:
            xs_copy_in(jz, jx)
            for jy in ys:
                launch(yf_copy(jz, jx, jy))
        for jy in ys:
            launch(near_copy(jz, 0, jy))
        for jx in xs:
            launch(near_copy(jz, jx, 0))

    def finish(jz):
        for jx in xs:
            for jy in ys:
                view = shard(jz, jx, jy, part, rest)
                remote(view, view, xf_sems, cross(jz, jx, jy), x_peers[jx]).wait_recv()
                view = shard(jz, jx, jy, 0, part)
                remote(view, view, yf_sems, cross(jz, jx, jy), y_peers[jy]).wait_recv()
                launch(near_copy(jz, jx, jy))

    def z_in(index):
        jz = z_order[index]
        view = shard(jz, 0, 0)
        remote(view, view, z_sems, jz - 1, z_peers[jz]).wait_recv()
        if index + 1 < zn:
            launch(z_copy(z_order[index + 1]))

    own_local = pltpu.make_async_copy(own, shard(0, 0, 0, 0, slots), own_sem)

    def begin():
        launch(z_copy(z_order[1]))
        send_own(0)
        own_local.start()
        if last:
            tail_begin()

    def advance(index):
        z_in(index)
        send_own(z_order[index])
        if last and index == 1:
            tail_across()

    def forward_step(index):
        forward(z_order[index])
        if last and index == zn - 2:
            tail_planes()

    def end():
        finish(z_order[zn - 1])
        if last:
            tail_end()
            tail_settle()
        for jz in range(zn):
            for jx in range(xn):
                for jy in range(yn):
                    chip = lax.div(number(jz, jx, jy), 2)
                    view = every.at[pl.ds((chip * 2 + 1 - core) * slots, count)]
                    remote(
                        view, view, near_sems, (jz * xn + jx) * yn + jy, core_peer
                    ).wait_recv()

    def settle():
        own_local.wait()
        for copy in started:
            copy.wait_send()

    steps = [begin]
    for index in range(1, zn):
        steps.append(functools.partial(advance, index))
        steps.append(functools.partial(forward_step, index - 1))
        if index >= 2:
            steps.append(functools.partial(finish, z_order[index - 2]))
    steps.append(functools.partial(forward_step, zn - 1))
    steps.append(functools.partial(finish, z_order[zn - 2]))
    steps.append(end)
    steps.append(settle)
    return [core_peer, *x_peers.values(), *y_peers.values(), *z_peers.values()], steps


def block_steps(sizes, pack, gathered, crossed, sems):
    zn, xn, yn = sizes
    by_sems, bz_sems, bx_sems, bn_sems, stay_sem = sems
    z, x = lax.axis_index("a"), lax.axis_index("b")
    y, core = lax.axis_index("y"), lax.axis_index("core")
    core_peer = {"core": 1 - core}
    xs, ys, z_order = range(1, xn), range(1, yn), z_order_of(zn)
    x_peers = {k: {"b": lax.rem(x + k, xn)} for k in xs}
    y_peers = {k: {"y": lax.rem(y + k, yn)} for k in ys}
    z_peers = {k: {"a": lax.rem(z + k, zn)} for k in range(1, zn)}
    hosts = lax.rem(z, 2) == core

    def block(jz, jx=0):
        return gathered.at[lax.rem(x + xn - jx, xn) * zn + lax.rem(z + zn - jz, zn)]

    def by_copy(jy):
        return remote(pack, crossed.at[jy - 1], by_sems, jy - 1, y_peers[jy])

    def plane(jy):
        return lax.rem(y + yn - jy, yn) * 2 + core

    def bz_copy(jy):
        src = pack if jy == 0 else crossed.at[jy - 1]
        far = lax.rem(plane(jy) + zn - z, zn)
        return remote(src, block(0), bz_sems, far, {"a": plane(jy)})

    def stay_copy(jy):
        src = pack if jy == 0 else crossed.at[jy - 1]
        return pltpu.make_async_copy(src, block(0), stay_sem)

    def bx_copy(jz, jx):
        return remote(block(jz), block(jz), bx_sems, jz * (xn - 1) + jx - 1, x_peers[jx])

    def bn_copy(jz, jx):
        return remote(block(jz, jx), block(jz, jx), bn_sems, jz * xn + jx, core_peer)

    def cross_y():
        for jy in ys:
            by_copy(jy).start()

    def to_planes():
        for jy in range(yn):
            if jy != 0:
                by_copy(jy).wait_recv()

            @pl.when(plane(jy) != z)
            def _():
                bz_copy(jy).start()

            @pl.when(plane(jy) == z)
            def _():
                stay_copy(jy).start()
                stay_copy(jy).wait()

    def across():
        @pl.when(hosts)
        def _():
            for jz in z_order:
                if jz != 0:
                    remote(block(jz), block(jz), bz_sems, jz, z_peers[jz]).wait_recv()
                for jx in xs:
                    bx_copy(jz, jx).start()
                bn_copy(jz, 0).start()

    def end():
        @pl.when(hosts)
        def _():
            for jz in z_order:
                for jx in xs:
                    view = block(jz, jx)
                    index = jz * (xn - 1) + jx - 1
                    remote(view, view, bx_sems, index, x_peers[jx]).wait_recv()
                    bn_copy(jz, jx).start()
            for jz in z_order:
                for jx in xs:
                    bx_copy(jz, jx).wait_send()
                for jx in range(xn):
                    bn_copy(jz, jx).wait_send()

        @pl.when(jnp.logical_not(hosts))
        def _():
            for jz in range(zn):
                for jx in range(xn):
                    bn_copy(jz, jx).wait_recv()

        for jy in range(yn):

            @pl.when(plane(jy) != z)
            def _():
                bz_copy(jy).wait_send()

        for jy in ys:
            by_copy(jy).wait_send()

    return [cross_y, to_planes, across, end]


def spread_kernel(
    sizes, master, x_in, seg_in, every, gathered, crossed, own, pack, *sems
):
    peers, steps = spread_steps(sizes, own, every, sems[:11])
    cross_y, to_planes, across, end = block_steps(sizes[:3], pack, gathered, crossed, sems[11:])
    tok, width = x_in.shape

    def prepare():
        own[...] = master[...].astype(BF16)
        pack[0:tok, :] = x_in[...]
        segs = jnp.concatenate(
            [seg_in[...].astype(F32), jnp.zeros((1, width - tok), F32)], axis=1
        )
        pack[tok:, :] = jnp.broadcast_to(segs, (pack.shape[0] - tok, width)).astype(BF16)

    greet(peers, meanwhile=prepare)
    steps[0]()
    cross_y()
    for step in steps[1:-7]:
        step()
    to_planes()
    for step in steps[-7:-3]:
        step()
    across()
    steps[-3]()
    steps[-2]()
    end()
    steps[-1]()


def reduce_steps(sizes, grads, total_out, refs):
    zn, xn, yn, slots, last = sizes
    held, near, xd, yd, xs_in, ys_in, zs_in, xb, yb, zb = refs[:10]
    load_sems, near_sems, xd_sems, yd_sems, xs_sems, ys_sems, zs_sems = refs[10:17]
    xb_sems, yb_sems, zb_sems = refs[17:20]
    count = slots - last
    part = count // 2
    rest = count - part
    tail = pl.ds(count, last)
    z, x = lax.axis_index("a"), lax.axis_index("b")
    y, core = lax.axis_index("y"), lax.axis_index("core")
    core_peer = {"core": 1 - core}
    xs, ys = range(1, xn), range(1, yn)
    y_peers = [{"y": lax.rem(y + k, yn)} for k in ys]
    x_peers = [{"b": lax.rem(x + k, xn)} for k in xs]
    z_peers = [{"a": lax.rem(z + k, zn)} for k in range(1, zn)]
    def flat(jz, jx, jy):
        return (jz * xn + jx) * yn + jy

    def chip_rows(jz, jx, jy, which):
        chip = (lax.rem(z + jz, zn) * xn + lax.rem(x + jx, xn)) * yn + lax.rem(y + jy, yn)
        return grads.at[pl.ds((chip * 2 + which) * slots, slots)]

    def near_copy(jz, jx, jy):
        index = flat(jz, jx, jy)
        return remote(chip_rows(jz, jx, jy, 1 - core), near.at[index], near_sems, index, core_peer)

    def load_copy(jz, jx, jy):
        index = flat(jz, jx, jy)
        return pltpu.make_async_copy(
            chip_rows(jz, jx, jy, core), held.at[index], load_sems.at[index]
        )

    def whole(jz, jx, jy):
        return held.at[flat(jz, jx, jy)]

    def first(jz, jx, jy):
        return held.at[flat(jz, jx, jy), pl.ds(0, part)]

    def second(jz, jx, jy):
        return held.at[flat(jz, jx, jy), pl.ds(part, rest)]

    def cross(jz, jx, jy):
        return (jz * (xn - 1) + jx - 1) * (yn - 1) + jy - 1

    def yd_copy(jz, jx, jy):
        index = cross(jz, jx, jy)
        return remote(first(jz, jx, jy), yd.at[index], yd_sems, index, y_peers[jy - 1])

    def xd_copy(jz, jx, jy):
        index = cross(jz, jx, jy)
        return remote(second(jz, jx, jy), xd.at[index], xd_sems, index, x_peers[jx - 1])

    def halves(low_half):
        return pl.ds(0, part) if low_half else pl.ds(part, rest)

    def xs_copy(jz, jx, low_half):
        index = jz * (xn - 1) + jx - 1
        return remote(
            held.at[flat(jz, jx, 0), halves(low_half)],
            xs_in.at[index, halves(low_half)],
            xs_sems,
            index * 2 + int(low_half),
            x_peers[jx - 1],
        )

    def ys_copy(jz, jy, low_half):
        index = jz * (yn - 1) + jy - 1
        return remote(
            held.at[flat(jz, 0, jy), halves(low_half)],
            ys_in.at[index, halves(low_half)],
            ys_sems,
            index * 2 + int(low_half),
            y_peers[jy - 1],
        )

    def zs_copy(jz):
        src = held.at[flat(jz, 0, 0), pl.ds(0, count)]
        return remote(src, zs_in.at[jz - 1], zs_sems, jz - 1, z_peers[jz - 1])

    def zb_copy(jz):
        src = held.at[pl.ds(jz * xn * yn, xn * yn), tail]
        return remote(src, zb.at[jz - 1], zb_sems, jz - 1, z_peers[jz - 1])

    def xb_copy(jx):
        src = held.at[pl.ds(jx * yn, yn), tail]
        return remote(src, xb.at[jx - 1], xb_sems, jx - 1, x_peers[jx - 1])

    def yb_copy(jy):
        return remote(held.at[jy, tail], yb.at[jy - 1], yb_sems, jy - 1, y_peers[jy - 1])

    def tail_planes():
        for jz in range(1, zn):
            zb_copy(jz).wait_recv()

        def one(i, carry):
            for chip in range(xn * yn):
                total = held[chip, count + i].astype(F32)
                for jz in range(1, zn):
                    total = total + zb[jz - 1, chip, i].astype(F32)
                held[chip, count + i] = total.astype(BF16)
            return carry

        lax.fori_loop(0, last, one, None)
        for jx in xs:
            launch(xb_copy(jx))

    def tail_columns():
        for jx in xs:
            xb_copy(jx).wait_recv()
            for jy in range(yn):
                add_low(held.at[jy, tail], xb.at[jx - 1, jy], last)
        for jy in ys:
            launch(yb_copy(jy))

    def tail_end():
        for jy in ys:
            yb_copy(jy).wait_recv()

        def one(i, carry):
            total = held[0, count + i].astype(F32)
            for jy in ys:
                total = total + yb[jy - 1, i].astype(F32)
            total_out[count + i] = total
            return carry

        lax.fori_loop(0, last, one, None)

    z_order = z_order_of(zn)[::-1]
    started = []

    def launch(copy):
        copy.start()
        started.append(copy)

    def plane(jz):
        return (
            [(jz, jx, jy) for jx in xs for jy in ys]
            + [(jz, jx, 0) for jx in xs]
            + [(jz, 0, jy) for jy in ys]
            + [(jz, 0, 0)]
        )

    def fetch(jz):
        for chip in plane(jz):
            launch(near_copy(*chip))
            load_copy(*chip).start()

    def prepare(index):
        for chip in plane(z_order[index]):
            load_copy(*chip).wait()
            near_copy(*chip).wait_recv()
            add_low(whole(*chip), near.at[flat(*chip)], slots)
        if index + 1 < zn:
            fetch(z_order[index + 1])
        if last and z_order[index] != 0:
            launch(zb_copy(z_order[index]))

    stages = [(index, stage) for index in range(zn) for stage in range(3)]

    def send_stage(number):
        index, stage = stages[number]
        jz = z_order[index]
        for jx in xs:
            if stage == 0:
                for jy in ys:
                    launch(xd_copy(jz, jx, jy))
            else:
                launch(xs_copy(jz, jx, stage == 2))
        for jy in ys:
            if stage == 0:
                for jx in xs:
                    launch(yd_copy(jz, jx, jy))
            else:
                launch(ys_copy(jz, jy, stage == 1))

    def take_stage(number):
        index, stage = stages[number]
        jz = z_order[index]
        if stage == 0:
            for jx in xs:
                for jy in ys:
                    yd_copy(jz, jx, jy).wait_recv()
                    add_low(first(jz, jx, 0), yd.at[cross(jz, jx, jy)], part)
                    xd_copy(jz, jx, jy).wait_recv()
                    add_low(second(jz, 0, jy), xd.at[cross(jz, jx, jy)], rest)
        else:
            for jx in xs:
                xs_copy(jz, jx, stage == 2).wait_recv()
            for jy in ys:
                ys_copy(jz, jy, stage == 1).wait_recv()

    def side_in(index):
        jz = z_order[index]

        def one(i, carry):
            total = held[flat(jz, 0, 0), i].astype(F32)
            for jx in xs:
                total = total + xs_in[jz * (xn - 1) + jx - 1, i].astype(F32)
            for jy in ys:
                total = total + ys_in[jz * (yn - 1) + jy - 1, i].astype(F32)
            if jz != 0:
                held[flat(jz, 0, 0), i] = total.astype(BF16)
            else:
                total_out[i] = total
            return carry

        lax.fori_loop(0, count, one, None)
        if jz != 0:
            launch(zs_copy(jz))

    ahead = 2

    def begin():
        fetch(z_order[0])

    def begin_stages():
        prepare(0)
        for number in range(ahead):
            send_stage(number)

    def one_stage(number):
        for index in range(1, zn):
            if number == (index - 1 if index < 3 else 3 * (index - 2)):
                prepare(index)
        take_stage(number)
        later = number + ahead
        if later < len(stages):
            send_stage(later)
        if stages[number][1] == 2:
            side_in(stages[number][0])
        if last and number == len(stages) - 4:
            tail_planes()
        if last and number == len(stages) - 2:
            tail_columns()

    def end():
        for jz in range(1, zn):
            zs_copy(jz).wait_recv()

        def add_planes(i, carry):
            total = total_out[i]
            for jz in range(1, zn):
                total = total + zs_in[jz - 1, i].astype(F32)
            total_out[i] = total
            return carry

        lax.fori_loop(0, count, add_planes, None)
        if last:
            tail_end()
        for copy in started:
            copy.wait_send()

    steps = [begin, begin_stages]
    steps += [functools.partial(one_stage, number) for number in range(len(stages))]
    steps.append(end)
    return [core_peer] + y_peers + x_peers + z_peers, steps


def reduce_kernel(sizes, grads, tokens_in, total_out, tokens_out, *refs):
    peers, steps = reduce_steps(sizes, grads, total_out, refs[:20])
    turn_sems = refs[20]
    greet(peers, True)
    turn_refs = (tokens_in, tokens_out, turn_sems.at[0], turn_sems.at[1])
    start_turn(*turn_refs)
    for step in steps:
        step()
    finish_turn(*turn_refs)


def vmem():
    return pl.BlockSpec(memory_space=pltpu.VMEM)


def smem():
    return pl.BlockSpec(memory_space=pltpu.SMEM)


def anywhere():
    return pl.BlockSpec(memory_space=pl.ANY)


def shape_of(dims, kind):
    return jax.ShapeDtypeStruct(dims, kind)


def params(collective=None):
    if collective is None:
        return pltpu.CompilerParams(vmem_limit_bytes=VMEM_LIMIT)
    return pltpu.CompilerParams(
        vmem_limit_bytes=VMEM_LIMIT, collective_id=collective, has_side_effects=True
    )


def pair(count):
    return pltpu.SemaphoreType.DMA((2, max(count, 1)))


def spread_scratch(zn, xn, yn):
    return [
        pair(zn - 1),
        pair(zn * (xn - 1)),
        pair(zn * (yn - 1)),
        pair(zn * (xn - 1) * (yn - 1)),
        pair(zn * (xn - 1) * (yn - 1)),
        pair(zn * xn * yn),
        pltpu.SemaphoreType.DMA,
        pair((xn - 1) * yn),
        pair(yn - 1),
        pair((zn - 1) * xn * yn),
        pair(zn * xn * yn),
    ]


def reduce_scratch(zn, xn, yn, slots, last, piece, width):
    def chunks(*dims):
        return pltpu.VMEM(tuple(max(dim, 1) for dim in dims) + (piece, width), BF16)

    n_chips, crossing = zn * xn * yn, zn * (xn - 1) * (yn - 1)
    count = slots - last
    part = count // 2
    return [
        chunks(n_chips, slots),
        chunks(n_chips, slots),
        chunks(crossing, count - part),
        chunks(crossing, part),
        chunks(zn * (xn - 1), count),
        chunks(zn * (yn - 1), count),
        chunks(zn - 1, count),
        chunks(xn - 1, yn, last),
        chunks(yn - 1, last),
        chunks(zn - 1, xn * yn, last),
        pltpu.SemaphoreType.DMA((n_chips,)),
        pair(n_chips),
        pair(crossing),
        pair(crossing),
        pair(2 * zn * (xn - 1)),
        pair(2 * zn * (yn - 1)),
        pair(zn - 1),
        pair(xn - 1),
        pair(yn - 1),
        pair(zn - 1),
    ]


def run_layer(dims, weight_master, x_own, segments, cotangent, location, norm_params):
    n_seq, n_dp = dims
    reps = n_seq // n_dp
    splits = n_seq // GROUPS
    slots, piece, width = weight_master.shape
    tok = cotangent.shape[0]
    length = tok * n_seq
    hidden_units = (location.shape[0] * piece - 4 * width) // 3
    head = width // HEADS
    kind_pieces = width // piece
    hidden_pieces = hidden_units // piece
    chunk = hidden_units // CHUNKS
    zn, xn, yn = n_dp, reps, n_dp // 2
    all_slots = n_seq * n_dp * slots
    last = slots // 8
    slopes = jnp.asarray(head_slopes(HEADS, tok, n_seq))

    weights, gathered, _ = pl.pallas_call(
        functools.partial(spread_kernel, (zn, xn, yn, slots, last)),
        out_shape=(
            shape_of((all_slots, piece, width), BF16),
            shape_of((n_seq, tok + 16, width), BF16),
            shape_of((max(yn - 1, 1), tok + 16, width), BF16),
        ),
        in_specs=[vmem(), vmem(), vmem()],
        out_specs=(anywhere(),) * 3,
        scratch_shapes=[
            pltpu.VMEM((slots, piece, width), BF16),
            pltpu.VMEM((tok + 16, width), BF16),
        ]
        + spread_scratch(zn, xn, yn)
        + [
            pair(yn - 1),
            pair(zn),
            pair(zn * (xn - 1)),
            pair(zn * xn),
            pltpu.SemaphoreType.DMA,
        ],
        compiler_params=params(1),
    )(weight_master, x_own, segments)
    attend_sizes = (n_dp, reps, splits, tok, head, n_seq)
    q_ext, k_ext, k_turned, v_rows, v_turned = pl.pallas_call(
        functools.partial(project_kernel, (n_dp, splits, tok, head)),
        grid=(n_seq,),
        out_shape=(
            shape_of((TRIO, GROUPS * tok, 128), BF16),
            shape_of((TRIO, length, 128), BF16),
            shape_of((TRIO, head, length), BF16),
            shape_of((TRIO, length, head), BF16),
            shape_of((TRIO, head, length), BF16),
        ),
        in_specs=[
            smem(),
            pl.BlockSpec((1, tok + 16, width), lambda i: (i, 0, 0)),
            anywhere(),
        ],
        out_specs=(
            pl.BlockSpec((TRIO, tok, 128), lambda i: (0, lax.div(i, splits), 0)),
            pl.BlockSpec((TRIO, tok, 128), lambda i: (0, i, 0)),
            pl.BlockSpec((TRIO, head, tok), lambda i: (0, 0, i)),
            pl.BlockSpec((TRIO, tok, head), lambda i: (0, i, 0)),
            pl.BlockSpec((TRIO, head, tok), lambda i: (0, 0, i)),
        ),
        scratch_shapes=[
            pltpu.VMEM((3 * TRIO, 128, width), BF16),
            pltpu.SemaphoreType.DMA((3 * TRIO * (head // piece),)),
        ],
        compiler_params=params(),
    )(location, gathered, weights)

    mixed_full, log_total, mixed_own, cotangent = pl.pallas_call(
        functools.partial(attend_forward_kernel, attend_sizes),
        out_shape=(
            shape_of((GROUPS, TRIO, head, tok), F32),
            shape_of((GROUPS, TRIO, 1, tok), F32),
            shape_of((GROUPS, TRIO, head, tok), BF16),
            shape_of(cotangent.shape, BF16),
        ),
        in_specs=[smem(), vmem(), vmem(), vmem(), anywhere()],
        out_specs=(vmem(), vmem(), vmem(), anywhere()),
        scratch_shapes=[
            pltpu.VMEM((3 * TRIO, tok, tok), F32),
            pltpu.VMEM((n_seq, tok, tok), F32),
            pltpu.VMEM((GROUPS, TRIO, head, tok), BF16),
            pair(GROUPS - 1),
            pltpu.SemaphoreType.DMA((2,)),
        ],
        compiler_params=params(2),
    )(slopes, q_ext, k_ext, v_turned, cotangent)

    out_low, d_pre_one, d_mixed, norm_part, grads = pl.pallas_call(
        functools.partial(
            dense_kernel, (n_dp, tok, piece, kind_pieces, chunk // piece, hidden_pieces)
        ),
        out_shape=(
            shape_of((tok, width), BF16),
            shape_of((tok, width), F32),
            shape_of((width, tok), BF16),
            shape_of((8, width), F32),
            shape_of((all_slots, piece, width), BF16),
        ),
        in_specs=[smem(), anywhere(), vmem(), vmem(), vmem(), anywhere()],
        out_specs=(vmem(), vmem(), vmem(), vmem(), anywhere()),
        scratch_shapes=[
            pltpu.VMEM((width, width), BF16),
            pltpu.VMEM((CHUNKS, chunk, width), BF16),
            pltpu.VMEM((CHUNKS, chunk, width), BF16),
            pltpu.VMEM((CHUNKS, chunk, width), BF16),
            pltpu.VMEM((CHUNKS, chunk, tok), F32),
            pltpu.VMEM((CHUNKS, chunk, tok), F32),
            pltpu.VMEM((CHUNKS, chunk, tok), BF16),
            pltpu.VMEM((2, 3, chunk, width), BF16),
            pltpu.VMEM((width, width), BF16),
            pltpu.VMEM((tok, width), BF16),
            pltpu.SemaphoreType.DMA((3 * CHUNKS + 1,)),
            pltpu.SemaphoreType.DMA((7,)),
            pltpu.SemaphoreType.DMA,
        ],
        compiler_params=params(),
    )(location, gathered, cotangent, mixed_own.reshape(width, tok), norm_params, weights)

    def norm_rows(count):
        return pltpu.VMEM((max(count, 1), 8, width), F32)

    d_own, result, norm_total = pl.pallas_call(
        functools.partial(attend_backward_kernel, attend_sizes),
        out_shape=(
            shape_of((GROUPS, 3, TRIO, head, tok), BF16),
            shape_of(out_low.shape, BF16),
            shape_of((8, width), F32),
        ),
        in_specs=[smem()] + [vmem()] * 7 + [anywhere(), vmem()],
        out_specs=(vmem(), anywhere(), vmem()),
        scratch_shapes=[
            pltpu.VMEM((length, 128), F32),
            pltpu.VMEM((length, head), F32),
            pltpu.VMEM((3 * TRIO, tok, tok), F32),
            pltpu.VMEM((GROUPS, TRIO, head, tok), BF16),
            pltpu.VMEM((GROUPS, 3, TRIO, head, tok), BF16),
            pltpu.VMEM((TRIO, splits, GROUPS, 2, head, tok), BF16),
            pltpu.VMEM((TRIO, splits - 1, GROUPS, 2, head, tok), BF16),
            pair(GROUPS - 1),
            pair(TRIO * (GROUPS - 1)),
            pair(TRIO * (splits - 1)),
            pair(TRIO * (GROUPS - 1)),
            pltpu.SemaphoreType.DMA((2,)),
            norm_rows(1),
            norm_rows(yn - 1),
            norm_rows(xn - 1),
            norm_rows(zn - 1),
            norm_rows(4),
            pair(1 + (yn - 1) + (xn - 1) + (zn - 1)),
        ],
        compiler_params=params(3),
    )(
        slopes,
        q_ext,
        k_ext,
        k_turned,
        v_rows,
        mixed_full,
        log_total,
        d_mixed.reshape(GROUPS, TRIO, head, tok),
        out_low,
        norm_part,
    )

    trio_rows = TRIO * head
    d_tokens, grads = pl.pallas_call(
        functools.partial(project_grad_kernel, (n_dp, tok, piece, kind_pieces)),
        out_shape=(shape_of((tok, width), BF16), shape_of(grads.shape, BF16)),
        in_specs=[smem(), anywhere(), vmem(), vmem()] + [anywhere()] * 2,
        out_specs=(vmem(), anywhere()),
        scratch_shapes=[
            pltpu.VMEM((GROUPS, 3 * trio_rows, width), BF16),
            pltpu.VMEM((GROUPS, 3 * trio_rows, width), BF16),
            pltpu.VMEM((tok, width), BF16),
            pltpu.SemaphoreType.DMA((GROUPS,)),
            pltpu.SemaphoreType.DMA((GROUPS,)),
            pltpu.SemaphoreType.DMA,
        ],
        input_output_aliases={5: 1},
        compiler_params=params(),
    )(location, gathered, d_own.reshape(GROUPS, 3 * trio_rows, tok), d_pre_one, weights, grads)

    own_grad, d_turned = pl.pallas_call(
        functools.partial(reduce_kernel, (zn, xn, yn, slots, last)),
        out_shape=(
            shape_of((slots, piece, width), F32),
            shape_of(d_tokens.shape, BF16),
        ),
        in_specs=[anywhere(), anywhere()],
        out_specs=(vmem(), anywhere()),
        scratch_shapes=reduce_scratch(zn, xn, yn, slots, last, piece, width)
        + [pltpu.SemaphoreType.DMA((2,))],
        compiler_params=params(4),
    )(grads, d_tokens)
    return own_grad, norm_total, d_turned, result


def per_device(
    dims,
    layer_input,
    out_cotangent,
    segment_ids,
    piece_owner,
    weight_master,
    weight_first,
    weight_second,
    norm_params,
    norm_first,
    norm_second,
):
    slots, piece, width = weight_master.shape
    pieces = piece_owner.shape[0]
    tok = layer_input.shape[1]
    hidden_units = (pieces * piece - 4 * width) // 3
    location = locate_pieces(piece_owner, slots)
    own_grad, norm_total, d_turned, result = run_layer(
        dims,
        weight_master,
        layer_input[0],
        segment_ids,
        out_cotangent[0],
        location,
        norm_params,
    )

    numbers = jnp.arange(pieces, dtype=jnp.int32) + 1
    own_slots = lax.axis_index(("a", "b", "y", "core")) * slots + jnp.arange(slots)
    inverse = jnp.sum(jnp.where(location[None, :] == own_slots[:, None], numbers[None, :], 0), axis=1)
    own_grad = jnp.where((inverse > 0)[:, None, None], own_grad, 0.0)
    norm_grad = norm_total[:4]
    rates = slot_rates(inverse, piece, width, hidden_units)
    first_new, second_new, weight_new = adamw_step(
        weight_master, weight_first, weight_second, own_grad, rates[:, None, None], STEP
    )
    norm_first_new, norm_second_new, norm_new = adamw_step(
        norm_params, norm_first, norm_second, norm_grad, NORM_RATE, STEP
    )
    return (
        result[None],
        d_turned.astype(F32)[None],
        own_grad,
        first_new,
        second_new,
        weight_new,
        weight_new.astype(BF16),
        norm_grad,
        norm_first_new,
        norm_second_new,
        norm_new,
    )


def solution(mesh):
    n_seq, n_dp = mesh.shape["seq"], mesh.shape["dp"]
    inner = Mesh(
        mesh.devices.reshape(n_dp, n_seq // n_dp, n_dp // 2, 2), ("a", "b", "y", "core")
    )
    seq, dp, every = ("a", "b"), ("y", "core"), ("a", "b", "y", "core")
    block = P(dp, seq, None)
    owned = P(every, None, None)
    in_specs = (block, block, P(dp, seq), P(), owned, owned, owned, P(), P(), P())
    out_specs = (block, block, owned, owned, owned, owned, owned, P(), P(), P(), P())
    return jax.shard_map(
        functools.partial(per_device, (n_seq, n_dp)),
        mesh=inner,
        in_specs=in_specs,
        out_specs=out_specs,
        check_vma=False,
    )
```

profile of v0, /device:TPU:8, one launch (start us, length us, event | category | flops | bytes accessed | tf_op | source)
XLA Modules:
  0.0 367.0 jit_solution(11613422585531321079)
XLA Ops:
  0.7 1.1 convert_reduce_fusion
  1.8 0.7 iota_add_fusion
  2.5 0.0 copy-start.3
  2.5 0.2 select_reduce_fusion
  2.7 121.4 %shard_map.194 = (bf16[1024,16,768]{2,1,0:T(8,128)(2,1)}, bf16[8,272,768]{2,1,0:T(8,128)(2,1)}, bf16[1,272,768]{2,1,0:T(8,128)(2,1)}) custom-call(f32[32,16,768]{2,1,0:T(8,128)} %master.1, bf16[256,768]{1,0:T(8,128)(2,1)} %bitcast.11, s32[1,256]{1,0:T(1,128)} %seg_in.1), custom_call_target="tpu_custom_call" | custom-call | tf_op jit(solution)/shard_map/pallas_call | solution.py:1497
  124.1 0.0 copy-done.3
  124.1 12.1 %shard_map.195 = (bf16[3,1024,128]{2,1,0:T(8,128)(2,1)}, bf16[3,2048,128]{2,1,0:T(8,128)(2,1)}, bf16[3,64,2048]{2,1,0:T(8,128)(2,1)}, bf16[3,2048,64]{2,1,0:T(8,128)(2,1)}, bf16[3,64,2048]{2,1,0:T(8,128)(2,1)}) custom-call(s32[768]{0:T(1024)} %copy-done.3, bf16[8,272,768]{2,1,0:T(8,128)(2,1)} %get-tuple-element.34.x_ref.gathered, ...), custom_call_target="tpu_custom_call" | custom-call | tf_op jit(solution)/shard_map/pallas_call | solution.py:1521
  136.2 25.1 %shard_map.196 = (f32[4,3,64,256]{3,2,1,0:T(8,128)}, f32[4,3,1,256]{3,2,1,0:T(1,128)}, bf16[4,3,64,256]{3,2,1,0:T(8,128)(2,1)}, bf16[256,768]{1,0:T(8,128)(2,1)}) custom-call(f32[12]{0:T(128)} %constant.67.clone.slopes, bf16[3,1024,128]{2,1,0:T(8,128)(2,1)} %get-tuple-element.36.q_ref, bf16[3,2048,128]{2,1,0:T(8,128)(2,1)} %get-tuple-element.37.k_ref, ...), custom_call_target="tpu_custom_call" | custom-call | tf_op jit(solution)/shard_map/pallas_call | solution.py:1550
  161.3 24.6 %shard_map.197 = (bf16[256,768]{1,0:T(8,128)(2,1)}, f32[256,768]{1,0:T(8,128)}, bf16[768,256]{1,0:T(8,128)(2,1)}, f32[8,768]{1,0:T(8,128)}, bf16[1024,16,768]{2,1,0:T(8,128)(2,1)}) custom-call(s32[768]{0:T(1024)} %copy-done.3, bf16[8,272,768]{2,1,0:T(8,128)(2,1)} %get-tuple-element.34.x_ref.gathered, bf16[256,768]{1,0:T(8,128)(2,1)} %get-tuple-element.43.cot_ref, ...), custom_call_target="tpu_custom_call" | custom-call | tf_op jit(solution)/shard_map/pallas_call | solution.py:1570
  185.9 46.4 %shard_map.198 = (bf16[4,3,3,64,256]{4,3,2,1,0:T(8,128)(2,1)}, bf16[256,768]{1,0:T(8,128)(2,1)}, f32[8,768]{1,0:T(8,128)}) custom-call(f32[12]{0:T(128)} %constant.67.clone.slopes, bf16[3,1024,128]{2,1,0:T(8,128)(2,1)} %get-tuple-element.36.q_ref, bf16[3,2048,128]{2,1,0:T(8,128)(2,1)} %get-tuple-element.37.k_ref, ...), custom_call_target="tpu_custom_call" | custom-call | tf_op jit(solution)/shard_map/pallas_call | solution.py:1604
  232.3 8.1 %shard_map.199 = (bf16[256,768]{1,0:T(8,128)(2,1)}, bf16[1024,16,768]{2,1,0:T(8,128)(2,1)}) custom-call(s32[768]{0:T(1024)} %copy-done.3, bf16[8,272,768]{2,1,0:T(8,128)(2,1)} %get-tuple-element.34.x_ref.gathered, bf16[4,576,256]{2,1,0:T(8,128)(2,1)} %bitcast.9, f32[256,768]{1,0:T(8,128)} %get-tuple-element.50.d_pre_one, ...), custom_call_target="tpu_custom_call", output_to_operand_aliasing={{1}: (5, {})} | custom-call | tf_op jit(solution)/shard_map/pallas_call | solution.py:1648
  240.5 0.0 copy-start.4
  240.5 0.0 copy-start.5
  240.5 0.0 copy-start.6
  240.5 0.0 copy-start.7
  240.5 0.0 copy-start
  240.5 0.0 copy-start.1
  240.5 117.3 %shard_map.200 = (f32[32,16,768]{2,1,0:T(8,128)}, bf16[256,768]{1,0:T(8,128)(2,1)}) custom-call(bf16[1024,16,768]{2,1,0:T(8,128)(2,1)} %get-tuple-element.52.grads, bf16[256,768]{1,0:T(8,128)(2,1)} %get-tuple-element.53.tokens_in), custom_call_target="tpu_custom_call" | custom-call | tf_op jit(solution)/shard_map/pallas_call | solution.py:1665
  357.8 0.0 copy-done.4
  357.8 0.0 copy-done.5
  357.8 0.0 copy-done.6
  357.9 0.0 copy-done.7
  357.9 0.6 multiply_subtract_fusion.1
  358.5 1.9 bitcast_convert_fusion
  360.4 0.0 copy-done
  360.4 0.0 copy-done.1
  360.4 0.0 copy-start.2
  360.4 5.8 %fusion.5 = (bf16[32,16,768]{2,1,0:T(8,128)(2,1)}, f32[32,16,768]{2,1,0:T(8,128)}, f32[32,16,768]{2,1,0:T(8,128)}, f32[32,16,768]{2,1,0:T(8,128)}, f32[32,16,768]{2,1,0:T(8,128)}) fusion(f32[32,16,768]{2,1,0:T(8,128)S(1)} %copy-done, f32[32]{0:T(128)S(1)} %fusion.3, f32[32,16,768]{2,1,0:T(8,128)S(1)} %copy-done.1, f32[32,16,768]{2,1,0:T(8,128)} %param.16, ...), kind=kLoop, calls=%fused_computation.22 | loop fusion | flops 6291456 | bytes 13369504 | tf_op jit(solution)/shard_map/convert_element_type | solution.py:1727
  366.2 0.0 copy-done.2
  366.2 0.7 copy.25
  (3 shorter events, 0.0 us)
Async XLA Ops:
  2.5 121.6 %copy-start.3 = (s32[768]{0:T(1024)}, s32[768]{0:T(1024)S(1)}, u32[]{:S(2)}) copy-start(s32[768]{0:T(1024)S(1)} %get-tuple-element.67.place) | copy-start | bytes 9220
  240.5 117.4 %copy-start.4 = (f32[4,768]{1,0:T(4,128)S(1)}, f32[4,768]{1,0:T(4,128)}, u32[]{:S(2)}) copy-start(f32[4,768]{1,0:T(4,128)} %norm_ref.1) | copy-start | bytes 36868
  240.5 117.4 %copy-start.5 = (f32[4,768]{1,0:T(4,128)S(1)}, f32[4,768]{1,0:T(4,128)}, u32[]{:S(2)}) copy-start(f32[4,768]{1,0:T(4,128)} %param.20) | copy-start | bytes 36868
  240.5 117.3 %copy-start.6 = (f32[4,768]{1,0:T(4,128)S(1)}, f32[4,768]{1,0:T(4,128)}, u32[]{:S(2)}) copy-start(f32[4,768]{1,0:T(4,128)} %param.19) | copy-start | bytes 36868
  240.5 117.3 %copy-start.7 = (f32[8,768]{1,0:T(8,128)S(1)}, f32[8,768]{1,0:T(8,128)}, u32[]{:S(2)}) copy-start(f32[8,768]{1,0:T(8,128)} %get-tuple-element.56) | copy-start | bytes 73732
  240.5 119.9 %copy-start = (f32[32,16,768]{2,1,0:T(8,128)S(1)}, f32[32,16,768]{2,1,0:T(8,128)}, u32[]{:S(2)}) copy-start(f32[32,16,768]{2,1,0:T(8,128)} %master.1) | copy-start | bytes 4718596
  240.5 119.9 %copy-start.1 = (f32[32,16,768]{2,1,0:T(8,128)S(1)}, f32[32,16,768]{2,1,0:T(8,128)}, u32[]{:S(2)}) copy-start(f32[32,16,768]{2,1,0:T(8,128)} %param.17) | copy-start | bytes 4718596
  360.4 5.8 %copy-start.2 = (bf16[256,768]{1,0:T(8,128)(2,1)S(1)}, bf16[256,768]{1,0:T(8,128)(2,1)}, u32[]{:S(2)}) copy-start(bf16[256,768]{1,0:T(8,128)(2,1)} %get-tuple-element.48) | copy-start | bytes 1179652
where the time goes:
time: 368 us; the launch traced here: 367 us
  Pallas kernels  355 us (96%)
  other arithmetic  10.4 us (3%)
    pallas_call x1, Pallas kernels, run_layer(): pl.pallas_call(functools.partial(spread_kernel, (zn, xn, yn, slots, last)...  121 us
    pallas_call x1, Pallas kernels, run_layer(): pl.pallas_call(functools.partial(reduce_kernel, (zn, xn, yn, slots, last)...  117 us
    pallas_call x1, Pallas kernels, run_layer(): pl.pallas_call(functools.partial(attend_backward_kernel, attend_sizes), o...  46.4 us
    pallas_call x1, Pallas kernels, run_layer(): pl.pallas_call(functools.partial(attend_forward_kernel, attend_sizes), ou...  25.1 us
    pallas_call x1, Pallas kernels, run_layer(): pl.pallas_call(functools.partial(dense_kernel, (n_dp, tok, piece, kind_pi...  24.6 us
    pallas_call x1, Pallas kernels, run_layer(): pl.pallas_call(functools.partial(project_kernel, (n_dp, splits, tok, head...  12.1 us
    pallas_call x1, Pallas kernels, run_layer(): pl.pallas_call(functools.partial(project_grad_kernel, (n_dp, tok, piece,...  8.14 us

commit v1 on v0

--- a/solution.py
+++ b/solution.py
@@ -303,15 +303,14 @@
         for kb in range(blocks):
             grown = jnp.exp(scores[kb] - (top + shifts[kb]))
             total = total + jnp.sum(grown, axis=0, keepdims=True)
-            scores[kb] = grown
-        inverse = 1.0 / total
+        log_total = top + jnp.log(total)
         mixed = jnp.zeros((head, tok), F32)
         for kb in range(blocks):
-            prob = (scores[kb] * inverse).astype(BF16)
+            prob = jnp.exp(scores[kb] - (log_total + shifts[kb])).astype(BF16)
             mixed = mixed + dot_nn(vt_ref[h, :, kb * tok : (kb + 1) * tok], prob)
         mixed_full[index, h] = mixed
         mixed_low[index, h] = mixed.astype(BF16)
-        log_out[index, h] = top + jnp.log(total)
+        log_out[index, h] = log_total
 
     for k in list(range(GROUPS - 1)) + [None]:
         index = group if k is None else others[k]
@@ -399,8 +398,7 @@
     own_ref,
     low_out,
     norm_out,
-    dk_sum,
-    dv_sum,
+    kv_sum,
     table,
     d_blocks,
     shared,
@@ -434,8 +432,7 @@
     d_blocks[group] = d_mixed[group]
     norms.pop(0)()
     fill_tables(table, slopes, group, tok)
-    dk_sum[...] = jnp.zeros_like(dk_sum)
-    dv_sum[...] = jnp.zeros_like(dv_sum)
+    kv_sum[...] = jnp.zeros_like(kv_sum)
 
     def step_fn(h, step):
         index = lax.rem(group + GROUPS - step, GROUPS)
@@ -451,6 +448,9 @@
         slope = slopes[group * TRIO + h]
         qh = q_ref[h, pl.ds(pl.multiple_of(index * tok, tok), tok), :]
         dt = d_blocks[index, h]
+        lane = lax.broadcasted_iota(jnp.int32, qh.shape, 1)
+        wide = jnp.concatenate([jnp.zeros((128 - head, tok), BF16), dt], axis=0)
+        both = jnp.concatenate([jnp.where(lane < head, qh, jnp.zeros_like(qh)), wide.T], axis=0)
         row_dot = jnp.sum(dt.astype(F32) * mixed_full[index, h], axis=0, keepdims=True)
         log_total = log_in[index, h]
         dq = jnp.zeros((head, tok), F32)
@@ -461,8 +461,8 @@
             prob = jnp.exp(now - (log_total + shift))
             d_prob = dot_nn(v_ref[h, rows, :], dt)
             d_score = (prob * (d_prob - row_dot)).astype(BF16)
-            dv_sum[rows, :] += dot_nt(prob.astype(BF16), dt)
-            dk_sum[rows, :] += dot_nn(d_score, qh)
+            sides = jnp.concatenate([d_score, prob.astype(BF16)], axis=1)
+            kv_sum[rows, :] += dot_nn(sides, both)
             dq = dq + dot_nn(kt_ref[h, :, rows], d_score)
         shared[index, 0, h] = (dq * (head**-0.5)).astype(BF16)
 
@@ -515,14 +515,14 @@
         def flip(index, carry, h=h):
             for part in range(splits):
                 rows = pl.ds(pl.multiple_of((index * splits + part) * tok, tok), tok)
-                pairs[h, part, index, 0] = dk_sum[rows, :].T[0:head].astype(BF16)
-                pairs[h, part, index, 1] = dv_sum[rows, :].T.astype(BF16)
+                flipped = kv_sum[rows, :].T.astype(BF16)
+                pairs[h, part, index, 0] = flipped[0:head]
+                pairs[h, part, index, 1] = flipped[128 - head :]
             return carry
 
         lax.fori_loop(0, GROUPS, flip, None)
         if h + 1 < TRIO:
-            dk_sum[...] = jnp.zeros_like(dk_sum)
-            dv_sum[...] = jnp.zeros_like(dv_sum)
+            kv_sum[...] = jnp.zeros_like(kv_sum)
         for k in range(splits - 1):
             launch(pair_copy(h, k))
         if h > 0:
@@ -1612,7 +1612,6 @@
         out_specs=(vmem(), anywhere(), vmem()),
         scratch_shapes=[
             pltpu.VMEM((length, 128), F32),
-            pltpu.VMEM((length, head), F32),
             pltpu.VMEM((3 * TRIO, tok, tok), F32),
             pltpu.VMEM((GROUPS, TRIO, head, tok), BF16),
             pltpu.VMEM((GROUPS, 3, TRIO, head, tok), BF16),

time: 368 us -> 380 us (1.033)
  Pallas kernels: 355 us -> 365 us
    pallas_call x1, Pallas kernels: 24.6 us -> 33.4 us  [run_layer(): pl.pallas_call(functools.partial(dense_kernel, (n_dp, tok, piece, kind_pi...]
where the time goes in v1:
time: 380 us; the launch traced here: 377 us
  Pallas kernels  365 us (96%)
  other arithmetic  10.4 us (3%)
    pallas_call x1, Pallas kernels, run_layer(): pl.pallas_call(functools.partial(spread_kernel, (zn, xn, yn, slots, last)...  121 us
    pallas_call x1, Pallas kernels, run_layer(): pl.pallas_call(functools.partial(reduce_kernel, (zn, xn, yn, slots, last)...  117 us
    pallas_call x1, Pallas kernels, run_layer(): pl.pallas_call(functools.partial(attend_backward_kernel, attend_sizes), o...  47.2 us
    pallas_call x1, Pallas kernels, run_layer(): pl.pallas_call(functools.partial(dense_kernel, (n_dp, tok, piece, kind_pi...  33.4 us
    pallas_call x1, Pallas kernels, run_layer(): pl.pallas_call(functools.partial(attend_forward_kernel, attend_sizes), ou...  25.7 us
    pallas_call x1, Pallas kernels, run_layer(): pl.pallas_call(functools.partial(project_kernel, (n_dp, splits, tok, head...  12.1 us
    pallas_call x1, Pallas kernels, run_layer(): pl.pallas_call(functools.partial(project_grad_kernel, (n_dp, tok, piece,...  8.14 us

profile of v1, /device:TPU:8, one launch (start us, length us, event | category | flops | bytes accessed | tf_op | source)
XLA Modules:
  0.0 377.1 jit_solution(3285253063973697036)
XLA Ops:
  0.7 1.1 convert_reduce_fusion
  1.8 0.7 iota_add_fusion
  2.5 0.0 copy-start.3
  2.5 0.2 select_reduce_fusion
  2.7 121.4 %shard_map.194 = (bf16[1024,16,768]{2,1,0:T(8,128)(2,1)}, bf16[8,272,768]{2,1,0:T(8,128)(2,1)}, bf16[1,272,768]{2,1,0:T(8,128)(2,1)}) custom-call(f32[32,16,768]{2,1,0:T(8,128)} %master.1, bf16[256,768]{1,0:T(8,128)(2,1)} %bitcast.11, s32[1,256]{1,0:T(1,128)} %seg_in.1), custom_call_target="tpu_custom_call" | custom-call | tf_op jit(solution)/shard_map/pallas_call | solution.py:1497
  124.1 0.0 copy-done.3
  124.1 12.1 %shard_map.195 = (bf16[3,1024,128]{2,1,0:T(8,128)(2,1)}, bf16[3,2048,128]{2,1,0:T(8,128)(2,1)}, bf16[3,64,2048]{2,1,0:T(8,128)(2,1)}, bf16[3,2048,64]{2,1,0:T(8,128)(2,1)}, bf16[3,64,2048]{2,1,0:T(8,128)(2,1)}) custom-call(s32[768]{0:T(1024)} %copy-done.3, bf16[8,272,768]{2,1,0:T(8,128)(2,1)} %get-tuple-element.34.x_ref.gathered, ...), custom_call_target="tpu_custom_call" | custom-call | tf_op jit(solution)/shard_map/pallas_call | solution.py:1521
  136.2 25.7 %shard_map.196 = (f32[4,3,64,256]{3,2,1,0:T(8,128)}, f32[4,3,1,256]{3,2,1,0:T(1,128)}, bf16[4,3,64,256]{3,2,1,0:T(8,128)(2,1)}, bf16[256,768]{1,0:T(8,128)(2,1)}) custom-call(f32[12]{0:T(128)} %constant.67.clone.slopes, bf16[3,1024,128]{2,1,0:T(8,128)(2,1)} %get-tuple-element.36.q_ref, bf16[3,2048,128]{2,1,0:T(8,128)(2,1)} %get-tuple-element.37.k_ref, ...), custom_call_target="tpu_custom_call" | custom-call | tf_op jit(solution)/shard_map/pallas_call | solution.py:1550
  161.9 33.4 %shard_map.197 = (bf16[256,768]{1,0:T(8,128)(2,1)}, f32[256,768]{1,0:T(8,128)}, bf16[768,256]{1,0:T(8,128)(2,1)}, f32[8,768]{1,0:T(8,128)}, bf16[1024,16,768]{2,1,0:T(8,128)(2,1)}) custom-call(s32[768]{0:T(1024)} %copy-done.3, bf16[8,272,768]{2,1,0:T(8,128)(2,1)} %get-tuple-element.34.x_ref.gathered, bf16[256,768]{1,0:T(8,128)(2,1)} %get-tuple-element.43.cot_ref, ...), custom_call_target="tpu_custom_call" | custom-call | tf_op jit(solution)/shard_map/pallas_call | solution.py:1570
  195.3 47.2 %shard_map.198 = (bf16[4,3,3,64,256]{4,3,2,1,0:T(8,128)(2,1)}, bf16[256,768]{1,0:T(8,128)(2,1)}, f32[8,768]{1,0:T(8,128)}) custom-call(f32[12]{0:T(128)} %constant.67.clone.slopes, bf16[3,1024,128]{2,1,0:T(8,128)(2,1)} %get-tuple-element.36.q_ref, bf16[3,2048,128]{2,1,0:T(8,128)(2,1)} %get-tuple-element.37.k_ref, ...), custom_call_target="tpu_custom_call" | custom-call | tf_op jit(solution)/shard_map/pallas_call | solution.py:1604
  242.5 8.1 %shard_map.199 = (bf16[256,768]{1,0:T(8,128)(2,1)}, bf16[1024,16,768]{2,1,0:T(8,128)(2,1)}) custom-call(s32[768]{0:T(1024)} %copy-done.3, bf16[8,272,768]{2,1,0:T(8,128)(2,1)} %get-tuple-element.34.x_ref.gathered, bf16[4,576,256]{2,1,0:T(8,128)(2,1)} %bitcast.9, f32[256,768]{1,0:T(8,128)} %get-tuple-element.50.d_pre_one, ...), custom_call_target="tpu_custom_call", output_to_operand_aliasing={{1}: (5, {})} | custom-call | tf_op jit(solution)/shard_map/pallas_call | solution.py:1647
  250.7 0.0 copy-start.4
  250.7 0.0 copy-start.5
  250.7 0.0 copy-start.6
  250.7 0.0 copy-start.7
  250.7 0.0 copy-start
  250.7 0.0 copy-start.1
  250.7 117.0 %shard_map.200 = (f32[32,16,768]{2,1,0:T(8,128)}, bf16[256,768]{1,0:T(8,128)(2,1)}) custom-call(bf16[1024,16,768]{2,1,0:T(8,128)(2,1)} %get-tuple-element.52.grads, bf16[256,768]{1,0:T(8,128)(2,1)} %get-tuple-element.53.tokens_in), custom_call_target="tpu_custom_call" | custom-call | tf_op jit(solution)/shard_map/pallas_call | solution.py:1664
  367.7 0.0 copy-done.4
  367.7 0.0 copy-done.5
  367.7 0.0 copy-done.6
  367.8 0.0 copy-done.7
  367.8 0.6 multiply_subtract_fusion.1
  368.4 1.9 bitcast_convert_fusion
  370.3 0.0 copy-done
  370.3 0.0 copy-done.1
  370.3 0.0 copy-start.2
  370.3 5.8 %fusion.5 = (bf16[32,16,768]{2,1,0:T(8,128)(2,1)}, f32[32,16,768]{2,1,0:T(8,128)}, f32[32,16,768]{2,1,0:T(8,128)}, f32[32,16,768]{2,1,0:T(8,128)}, f32[32,16,768]{2,1,0:T(8,128)}) fusion(f32[32,16,768]{2,1,0:T(8,128)S(1)} %copy-done, f32[32]{0:T(128)S(1)} %fusion.3, f32[32,16,768]{2,1,0:T(8,128)S(1)} %copy-done.1, f32[32,16,768]{2,1,0:T(8,128)} %param.16, ...), kind=kLoop, calls=%fused_computation.22 | loop fusion | flops 6291456 | bytes 13369504 | tf_op jit(solution)/shard_map/convert_element_type | solution.py:1726
  376.1 0.0 copy-done.2
  376.1 0.7 copy.25
  (3 shorter events, 0.0 us)
Async XLA Ops:
  2.5 121.6 %copy-start.3 = (s32[768]{0:T(1024)}, s32[768]{0:T(1024)S(1)}, u32[]{:S(2)}) copy-start(s32[768]{0:T(1024)S(1)} %get-tuple-element.67.place) | copy-start | bytes 9220
  250.7 117.0 %copy-start.4 = (f32[4,768]{1,0:T(4,128)S(1)}, f32[4,768]{1,0:T(4,128)}, u32[]{:S(2)}) copy-start(f32[4,768]{1,0:T(4,128)} %norm_ref.1) | copy-start | bytes 36868
  250.7 117.0 %copy-start.5 = (f32[4,768]{1,0:T(4,128)S(1)}, f32[4,768]{1,0:T(4,128)}, u32[]{:S(2)}) copy-start(f32[4,768]{1,0:T(4,128)} %param.20) | copy-start | bytes 36868
  250.7 117.0 %copy-start.6 = (f32[4,768]{1,0:T(4,128)S(1)}, f32[4,768]{1,0:T(4,128)}, u32[]{:S(2)}) copy-start(f32[4,768]{1,0:T(4,128)} %param.19) | copy-start | bytes 36868
  250.7 117.0 %copy-start.7 = (f32[8,768]{1,0:T(8,128)S(1)}, f32[8,768]{1,0:T(8,128)}, u32[]{:S(2)}) copy-start(f32[8,768]{1,0:T(8,128)} %get-tuple-element.56) | copy-start | bytes 73732
  250.7 119.6 %copy-start = (f32[32,16,768]{2,1,0:T(8,128)S(1)}, f32[32,16,768]{2,1,0:T(8,128)}, u32[]{:S(2)}) copy-start(f32[32,16,768]{2,1,0:T(8,128)} %master.1) | copy-start | bytes 4718596
  250.7 119.6 %copy-start.1 = (f32[32,16,768]{2,1,0:T(8,128)S(1)}, f32[32,16,768]{2,1,0:T(8,128)}, u32[]{:S(2)}) copy-start(f32[32,16,768]{2,1,0:T(8,128)} %param.17) | copy-start | bytes 4718596
  370.3 5.8 %copy-start.2 = (bf16[256,768]{1,0:T(8,128)(2,1)S(1)}, bf16[256,768]{1,0:T(8,128)(2,1)}, u32[]{:S(2)}) copy-start(bf16[256,768]{1,0:T(8,128)(2,1)} %get-tuple-element.48) | copy-start | bytes 1179652

commit v2 on v0

--- a/solution.py
+++ b/solution.py
@@ -1491,7 +1491,7 @@
     chunk = hidden_units // CHUNKS
     zn, xn, yn = n_dp, reps, n_dp // 2
     all_slots = n_seq * n_dp * slots
-    last = slots // 8
+    last, reduce_last = slots // 8, slots * 3 // 32
     slopes = jnp.asarray(head_slopes(HEADS, tok, n_seq))
 
     weights, gathered, _ = pl.pallas_call(
@@ -1663,14 +1663,14 @@
     )(location, gathered, d_own.reshape(GROUPS, 3 * trio_rows, tok), d_pre_one, weights, grads)
 
     own_grad, d_turned = pl.pallas_call(
-        functools.partial(reduce_kernel, (zn, xn, yn, slots, last)),
+        functools.partial(reduce_kernel, (zn, xn, yn, slots, reduce_last)),
         out_shape=(
             shape_of((slots, piece, width), F32),
             shape_of(d_tokens.shape, BF16),
         ),
         in_specs=[anywhere(), anywhere()],
         out_specs=(vmem(), anywhere()),
-        scratch_shapes=reduce_scratch(zn, xn, yn, slots, last, piece, width)
+        scratch_shapes=reduce_scratch(zn, xn, yn, slots, reduce_last, piece, width)
         + [pltpu.SemaphoreType.DMA((2,))],
         compiler_params=params(4),
     )(grads, d_tokens)

time: 368 us -> 363 us (0.986)
  Pallas kernels: 355 us -> 349 us
    pallas_call x1, Pallas kernels: 117 us -> 111 us  [run_layer(): pl.pallas_call(functools.partial(reduce_kernel, (zn, xn, yn, slots, reduc...]
where the time goes in v2:
time: 363 us; the launch traced here: 361 us
  Pallas kernels  349 us (96%)
  other arithmetic  10.4 us (3%)
    pallas_call x1, Pallas kernels, run_layer(): pl.pallas_call(functools.partial(spread_kernel, (zn, xn, yn, slots, last)...  121 us
    pallas_call x1, Pallas kernels, run_layer(): pl.pallas_call(functools.partial(reduce_kernel, (zn, xn, yn, slots, reduc...  111 us
    pallas_call x1, Pallas kernels, run_layer(): pl.pallas_call(functools.partial(attend_backward_kernel, attend_sizes), o...  46.4 us
    pallas_call x1, Pallas kernels, run_layer(): pl.pallas_call(functools.partial(attend_forward_kernel, attend_sizes), ou...  25.1 us
    pallas_call x1, Pallas kernels, run_layer(): pl.pallas_call(functools.partial(dense_kernel, (n_dp, tok, piece, kind_pi...  24.6 us
    pallas_call x1, Pallas kernels, run_layer(): pl.pallas_call(functools.partial(project_kernel, (n_dp, splits, tok, head...  12.1 us
    pallas_call x1, Pallas kernels, run_layer(): pl.pallas_call(functools.partial(project_grad_kernel, (n_dp, tok, piece,...  8.14 us

profile of v2, /device:TPU:8, one launch (start us, length us, event | category | flops | bytes accessed | tf_op | source)
XLA Modules:
  0.0 360.6 jit_solution(17866255606663357686)
XLA Ops:
  0.7 1.1 convert_reduce_fusion
  1.8 0.7 iota_add_fusion
  2.5 0.0 copy-start.3
  2.5 0.2 select_reduce_fusion
  2.7 121.4 %shard_map.194 = (bf16[1024,16,768]{2,1,0:T(8,128)(2,1)}, bf16[8,272,768]{2,1,0:T(8,128)(2,1)}, bf16[1,272,768]{2,1,0:T(8,128)(2,1)}) custom-call(f32[32,16,768]{2,1,0:T(8,128)} %master.1, bf16[256,768]{1,0:T(8,128)(2,1)} %bitcast.11, s32[1,256]{1,0:T(1,128)} %seg_in.1), custom_call_target="tpu_custom_call" | custom-call | tf_op jit(solution)/shard_map/pallas_call | solution.py:1497
  124.1 0.0 copy-done.3
  124.1 12.1 %shard_map.195 = (bf16[3,1024,128]{2,1,0:T(8,128)(2,1)}, bf16[3,2048,128]{2,1,0:T(8,128)(2,1)}, bf16[3,64,2048]{2,1,0:T(8,128)(2,1)}, bf16[3,2048,64]{2,1,0:T(8,128)(2,1)}, bf16[3,64,2048]{2,1,0:T(8,128)(2,1)}) custom-call(s32[768]{0:T(1024)} %copy-done.3, bf16[8,272,768]{2,1,0:T(8,128)(2,1)} %get-tuple-element.34.x_ref.gathered, ...), custom_call_target="tpu_custom_call" | custom-call | tf_op jit(solution)/shard_map/pallas_call | solution.py:1521
  136.2 25.1 %shard_map.196 = (f32[4,3,64,256]{3,2,1,0:T(8,128)}, f32[4,3,1,256]{3,2,1,0:T(1,128)}, bf16[4,3,64,256]{3,2,1,0:T(8,128)(2,1)}, bf16[256,768]{1,0:T(8,128)(2,1)}) custom-call(f32[12]{0:T(128)} %constant.67.clone.slopes, bf16[3,1024,128]{2,1,0:T(8,128)(2,1)} %get-tuple-element.36.q_ref, bf16[3,2048,128]{2,1,0:T(8,128)(2,1)} %get-tuple-element.37.k_ref, ...), custom_call_target="tpu_custom_call" | custom-call | tf_op jit(solution)/shard_map/pallas_call | solution.py:1550
  161.3 24.6 %shard_map.197 = (bf16[256,768]{1,0:T(8,128)(2,1)}, f32[256,768]{1,0:T(8,128)}, bf16[768,256]{1,0:T(8,128)(2,1)}, f32[8,768]{1,0:T(8,128)}, bf16[1024,16,768]{2,1,0:T(8,128)(2,1)}) custom-call(s32[768]{0:T(1024)} %copy-done.3, bf16[8,272,768]{2,1,0:T(8,128)(2,1)} %get-tuple-element.34.x_ref.gathered, bf16[256,768]{1,0:T(8,128)(2,1)} %get-tuple-element.43.cot_ref, ...), custom_call_target="tpu_custom_call" | custom-call | tf_op jit(solution)/shard_map/pallas_call | solution.py:1570
  185.9 46.4 %shard_map.198 = (bf16[4,3,3,64,256]{4,3,2,1,0:T(8,128)(2,1)}, bf16[256,768]{1,0:T(8,128)(2,1)}, f32[8,768]{1,0:T(8,128)}) custom-call(f32[12]{0:T(128)} %constant.67.clone.slopes, bf16[3,1024,128]{2,1,0:T(8,128)(2,1)} %get-tuple-element.36.q_ref, bf16[3,2048,128]{2,1,0:T(8,128)(2,1)} %get-tuple-element.37.k_ref, ...), custom_call_target="tpu_custom_call" | custom-call | tf_op jit(solution)/shard_map/pallas_call | solution.py:1604
  232.3 8.1 %shard_map.199 = (bf16[256,768]{1,0:T(8,128)(2,1)}, bf16[1024,16,768]{2,1,0:T(8,128)(2,1)}) custom-call(s32[768]{0:T(1024)} %copy-done.3, bf16[8,272,768]{2,1,0:T(8,128)(2,1)} %get-tuple-element.34.x_ref.gathered, bf16[4,576,256]{2,1,0:T(8,128)(2,1)} %bitcast.9, f32[256,768]{1,0:T(8,128)} %get-tuple-element.50.d_pre_one, ...), custom_call_target="tpu_custom_call", output_to_operand_aliasing={{1}: (5, {})} | custom-call | tf_op jit(solution)/shard_map/pallas_call | solution.py:1648
  240.5 0.0 copy-start.4
  240.5 0.0 copy-start.5
  240.5 0.0 copy-start.6
  240.5 0.0 copy-start.7
  240.5 0.0 copy-start
  240.5 0.0 copy-start.1
  240.5 110.9 %shard_map.200 = (f32[32,16,768]{2,1,0:T(8,128)}, bf16[256,768]{1,0:T(8,128)(2,1)}) custom-call(bf16[1024,16,768]{2,1,0:T(8,128)(2,1)} %get-tuple-element.52.grads, bf16[256,768]{1,0:T(8,128)(2,1)} %get-tuple-element.53.tokens_in), custom_call_target="tpu_custom_call" | custom-call | tf_op jit(solution)/shard_map/pallas_call | solution.py:1665
  351.5 0.0 copy-done.4
  351.5 0.0 copy-done.5
  351.5 0.0 copy-done.6
  351.5 0.0 copy-done.7
  351.5 0.6 multiply_subtract_fusion.1
  352.1 1.9 bitcast_convert_fusion
  354.1 0.0 copy-done
  354.1 0.0 copy-done.1
  354.1 0.0 copy-start.2
  354.1 5.8 %fusion.5 = (bf16[32,16,768]{2,1,0:T(8,128)(2,1)}, f32[32,16,768]{2,1,0:T(8,128)}, f32[32,16,768]{2,1,0:T(8,128)}, f32[32,16,768]{2,1,0:T(8,128)}, f32[32,16,768]{2,1,0:T(8,128)}) fusion(f32[32,16,768]{2,1,0:T(8,128)S(1)} %copy-done, f32[32]{0:T(128)S(1)} %fusion.3, f32[32,16,768]{2,1,0:T(8,128)S(1)} %copy-done.1, f32[32,16,768]{2,1,0:T(8,128)} %param.16, ...), kind=kLoop, calls=%fused_computation.22 | loop fusion | flops 6291456 | bytes 13369504 | tf_op jit(solution)/shard_map/convert_element_type | solution.py:1727
  359.9 0.0 copy-done.2
  359.9 0.7 copy.25
  (3 shorter events, 0.0 us)
Async XLA Ops:
  2.5 121.6 %copy-start.3 = (s32[768]{0:T(1024)}, s32[768]{0:T(1024)S(1)}, u32[]{:S(2)}) copy-start(s32[768]{0:T(1024)S(1)} %get-tuple-element.67.place) | copy-start | bytes 9220
  240.5 111.0 %copy-start.4 = (f32[4,768]{1,0:T(4,128)S(1)}, f32[4,768]{1,0:T(4,128)}, u32[]{:S(2)}) copy-start(f32[4,768]{1,0:T(4,128)} %norm_ref.1) | copy-start | bytes 36868
  240.5 111.0 %copy-start.5 = (f32[4,768]{1,0:T(4,128)S(1)}, f32[4,768]{1,0:T(4,128)}, u32[]{:S(2)}) copy-start(f32[4,768]{1,0:T(4,128)} %param.20) | copy-start | bytes 36868
  240.5 111.0 %copy-start.6 = (f32[4,768]{1,0:T(4,128)S(1)}, f32[4,768]{1,0:T(4,128)}, u32[]{:S(2)}) copy-start(f32[4,768]{1,0:T(4,128)} %param.19) | copy-start | bytes 36868
  240.5 111.0 %copy-start.7 = (f32[8,768]{1,0:T(8,128)S(1)}, f32[8,768]{1,0:T(8,128)}, u32[]{:S(2)}) copy-start(f32[8,768]{1,0:T(8,128)} %get-tuple-element.56) | copy-start | bytes 73732
  240.5 113.6 %copy-start = (f32[32,16,768]{2,1,0:T(8,128)S(1)}, f32[32,16,768]{2,1,0:T(8,128)}, u32[]{:S(2)}) copy-start(f32[32,16,768]{2,1,0:T(8,128)} %master.1) | copy-start | bytes 4718596
  240.5 113.5 %copy-start.1 = (f32[32,16,768]{2,1,0:T(8,128)S(1)}, f32[32,16,768]{2,1,0:T(8,128)}, u32[]{:S(2)}) copy-start(f32[32,16,768]{2,1,0:T(8,128)} %param.17) | copy-start | bytes 4718596
  354.1 5.8 %copy-start.2 = (bf16[256,768]{1,0:T(8,128)(2,1)S(1)}, bf16[256,768]{1,0:T(8,128)(2,1)}, u32[]{:S(2)}) copy-start(bf16[256,768]{1,0:T(8,128)(2,1)} %get-tuple-element.48) | copy-start | bytes 1179652
